TPU v7x, 32 devices: a whole 2x2x4 slice. The times are simulated.
32 devices in a mesh: node: 4 (over y, core), tm: 8 (over z, x).
Axes of the slice: x: 2, y: 2, z: 4, core: 2. Of those that a mesh axis runs over, the one named last changes fastest.
Arguments:
- memory: bfloat16 [32768, 1024], P(('node', 'tm')), may hold values from -6 to 6
- ends_owner: int32 [8192, 2], P(('node', 'tm')), may hold values from 0 to 31, all different within a row; in each aligned block of 256 rows (0 to 255, 256 to 511, ...) at most 20 rows name the same one
- ends_row: int32 [8192, 2], P(('node', 'tm')), may hold values from 0 to 1023
- event_mask: int32 [8192], P(('node', 'tm')), may hold values 0 or 1
- edge_feat: bfloat16 [8192, 128], P(('node', 'tm')), may hold values from -6 to 6
- msg_w1: bfloat16 [2176, 1024], replicated, may hold values from -0.125 to 0.125
- msg_b1: float32 [1024], replicated, may hold values from -4 to 4
- msg_w2: bfloat16 [1024, 1024], replicated, may hold values from -0.1875 to 0.1875
- msg_b2: float32 [1024], replicated, may hold values from -3 to 3
- gru_in: bfloat16 [1024, 3072], replicated, may hold values from -0.1875 to 0.1875
- gru_hid: bfloat16 [1024, 3072], replicated, may hold values from -0.1875 to 0.1875
- gru_bias: float32 [3072], replicated, may hold values from -3 to 3
Outputs:
- new_memory: bfloat16 [32768, 1024], P(('node', 'tm'))
Inputs may be any that keep to these rules, and one draw needn't show every extreme that they name: `ends_owner`: within the events of one device (aligned blocks of 256 rows) no device is named by more than 20 endpoints, and some device by exactly 20; an event's two endpoints have different owners.
All inputs are finite; a program needn't handle non-finite values. No bound on the sum of `event_mask` on one device may be relied on, other than what follows from the above.
Results may differ from a plain program's by a relative error of at most 0.0026.
Values may be sent and summed in bfloat16 or wider, within the bound.
A program may use at most 128 MiB of HBM per device.

v0:
```python
import jax
import jax.numpy as jnp
from jax import lax
from jax.sharding import PartitionSpec as P


def memory_update(aggregate, memory, gru_in, gru_hid, gru_bias, touched):
    feature_width = memory.shape[1]
    gates_in = jnp.dot(aggregate, gru_in, preferred_element_type=jnp.float32) + gru_bias
    gates_hid = jnp.dot(memory, gru_hid, preferred_element_type=jnp.float32)
    reset = jax.nn.sigmoid(gates_in[:, :feature_width] + gates_hid[:, :feature_width])
    update = jax.nn.sigmoid(
        gates_in[:, feature_width : 2 * feature_width]
        + gates_hid[:, feature_width : 2 * feature_width]
    )
    candidate = jnp.tanh(
        gates_in[:, 2 * feature_width :] + reset * gates_hid[:, 2 * feature_width :]
    )
    previous = memory.astype(jnp.float32)
    renewed = (1.0 - update) * candidate + update * previous
    return jnp.where(touched[:, None], renewed, previous).astype(jnp.bfloat16)


def on_device(
    memory,
    ends_owner,
    ends_row,
    event_mask,
    edge_feat,
    msg_w1,
    msg_b1,
    msg_w2,
    msg_b2,
    gru_in,
    gru_hid,
    gru_bias,
):
    devices = lax.axis_size(("node", "tm"))
    events = ends_owner.shape[0]
    feature_width = memory.shape[1]
    capacity = 5 * events // (2 * devices)
    slot_count = devices * capacity
    owners = ends_owner.reshape(-1)
    wanted = ends_row.reshape(-1)
    onehot = (owners[:, None] == jnp.arange(devices, dtype=jnp.int32)[None, :]).astype(jnp.int32)
    position = jnp.sum((jnp.cumsum(onehot, axis=0) - 1) * onehot, axis=1)
    location = owners * capacity + position
    requests = (
        jnp.zeros((slot_count,), jnp.int32).at[location].set(wanted).reshape(devices, capacity)
    )
    arrived = lax.all_to_all(requests, ("node", "tm"), split_axis=0, concat_axis=0, tiled=True)
    flat_ids = arrived.reshape(-1)
    answers = jnp.take(memory, flat_ids, axis=0)
    returned = lax.all_to_all(
        answers.reshape(devices, capacity, feature_width),
        ("node", "tm"),
        split_axis=0,
        concat_axis=0,
        tiled=True,
    )
    fetched = jnp.take(returned.reshape(slot_count, feature_width), location, axis=0).reshape(
        events, 2 * feature_width
    )
    inputs = jnp.concatenate([fetched, edge_feat], axis=1)
    hidden = jax.nn.relu(
        jnp.dot(inputs, msg_w1, preferred_element_type=jnp.float32) + msg_b1
    ).astype(jnp.bfloat16)
    weight_mask = event_mask.astype(jnp.float32)
    message = (
        (jnp.dot(hidden, msg_w2, preferred_element_type=jnp.float32) + msg_b2)
        * weight_mask[:, None]
    ).astype(jnp.bfloat16)
    target = location.reshape(events, 2)[:, 1]
    outgoing = jnp.zeros((slot_count, feature_width), jnp.bfloat16).at[target].set(message)
    tallies = jnp.zeros((slot_count,), jnp.bfloat16).at[target].set(event_mask.astype(jnp.bfloat16))
    incoming, counted = (
        lax.all_to_all(
            outgoing.reshape(devices, capacity, feature_width),
            ("node", "tm"),
            split_axis=0,
            concat_axis=0,
            tiled=True,
        ),
        lax.all_to_all(
            tallies.reshape(devices, capacity),
            ("node", "tm"),
            split_axis=0,
            concat_axis=0,
            tiled=True,
        ),
    )
    mates = (flat_ids[:, None] == flat_ids[None, :]).astype(jnp.bfloat16)
    summed = jnp.dot(
        mates, incoming.reshape(slot_count, feature_width), preferred_element_type=jnp.float32
    )
    tally_sum = jnp.dot(mates, counted.reshape(slot_count), preferred_element_type=jnp.float32)
    aggregate = (summed / jnp.maximum(tally_sum, 1.0)[:, None]).astype(jnp.bfloat16)
    renewed = memory_update(aggregate, answers, gru_in, gru_hid, gru_bias, tally_sum > 0.5)
    return memory.at[flat_ids].set(renewed)


def solution(mesh):
    return jax.shard_map(
        on_device,
        mesh=mesh,
        in_specs=(
            P(("node", "tm"), None),
            P(("node", "tm"), None),
            P(("node", "tm"), None),
            P(("node", "tm")),
            P(("node", "tm"), None),
            P(),
            P(),
            P(),
            P(),
            P(),
            P(),
            P(),
        ),
        out_specs=P(("node", "tm"), None),
        check_vma=False,
    )
```

profile of v0, /device:TPU:0, one launch (start us, length us, event | category | flops | bytes accessed | tf_op | source)
XLA Modules:
  0.0 173.7 jit_solution(10342762168905644378)
XLA Ops:
  0.0 3.2 %copy.54 = bf16[1024,1024]{1,0:T(8,128)(2,1)} copy(bf16[1024,1024]{1,0:T(8,128)(2,1)} %param.12) | data formatting | bytes 4194304
  6.4 2.4 %scatter_custom_fusion = s32[640]{0:T(1024)S(1)} fusion(s32[512]{0:T(512)S(1)} %bitcast.37, s32[512]{0:T(512)S(1)} %reshape.169, s32[]{:T(128)} %constant.18.clone.1), kind=kCustom, calls=%fused_computation.75 | custom fusion | bytes 2564 | tf_op jit(solution)/shard_map/scatter | solution.py:49
  9.0 14.2 %all_to_all.29 = s32[32,1,20]{2,1,0:T(1,128)S(1)} all-to-all(s32[32,1,20]{2,1,0:T(1,128)S(1)} %bitcast.35), channel_id=1, replica_groups=mesh['node'=4,'tm'=8] {'node','tm'}, dimensions={0} | all-to-all | bytes 5120 | tf_op jit(solution)/shard_map/all_to_all | solution.py:51
  24.7 5.7 %gather_fusion = bf16[640,1024]{1,0:T(8,128)(2,1)S(1)} fusion(bf16[1024,1024]{1,0:T(8,128)(2,1)} %copy.54, s32[1024]{0:T(1024)S(1)} %pad_clamp_fusion.1), kind=kCustom, calls=%fused_computation | custom fusion | bytes 2624000 | tf_op jit(solution)/shard_map/jit(_take)/gather | solution.py:53
  30.5 1.4 gather.13
  31.9 2.8 %broadcast_select_fusion = bf16[32,20,1024]{2,1,0:T(8,128)(2,1)} fusion(bf16[32,20,1024]{2,1,0:T(8,128)(2,1)} %gather.13, pred[32,20]{1,0:T(8,128)(4,1)S(1)} %compare_and_fusion), kind=kLoop, calls=%fused_computation.31 | loop fusion | flops 655360 | bytes 2622080 | tf_op jit(solution)/shard_map/jit(_take)/select_n | solution.py:53
  34.6 3.6 %all-to-all-start.2 = ((bf16[32,20,1024]{2,1,0:T(8,128)(2,1)}), bf16[32,20,1024]{2,1,0:T(8,128)(2,1)}, u32[]{:S(2)}, u32[]{:S(2)}) async-start(bf16[32,20,1024]{2,1,0:T(8,128)(2,1)} %broadcast_select_fusion), calls=%async_computation.2 | async-start | bytes 3145728 | tf_op jit(solution)/shard_map/all_to_all | solution.py:54
  40.0 2.2 %scatter_custom_fusion.1 = bf16[640]{0:T(1024)(128)(2,1)S(1)} fusion(s32[256]{0:T(256)S(1)} %bitcast.39, bf16[256]{0:T(256)(128)(2,1)S(1)} %get-tuple-element.7, bf16[]{:T(256)} %constant.29.clone.1), kind=kCustom, calls=%fused_computation.77 | custom fusion | bytes 1282 | tf_op jit(solution)/shard_map/scatter | solution.py:75
  43.6 33.4 %all-to-all-done.2 = bf16[32,20,1024]{2,1,0:T(8,128)(2,1)} async-done(((bf16[32,20,1024]{2,1,0:T(8,128)(2,1)}), bf16[32,20,1024]{2,1,0:T(8,128)(2,1)}, u32[]{:S(2)}, u32[]{:S(2)}) %all-to-all-start.2) | async-done | bytes 1310752 | tf_op jit(solution)/shard_map/all_to_all | solution.py:54
  77.0 2.5 %all-to-all-start.1 = ((bf16[32,1,20]{2,1,0:T(2,128)(2,1)}), bf16[32,1,20]{2,1,0:T(2,128)(2,1)S(1)}, u32[]{:S(2)}, u32[]{:S(2)}) async-start(bf16[32,1,20]{2,1,0:T(2,128)(2,1)} %all_to_all.24), calls=%async_computation.1 | async-start | bytes 32768 | tf_op jit(solution)/shard_map/all_to_all | solution.py:84
  79.5 2.3 %reshape.146 = bf16[640,1024]{1,0:T(8,128)(2,1)S(1)} reshape(bf16[32,20,1024]{2,1,0:T(8,128)(2,1)} %all-to-all-done.2) | data formatting | bytes 2621440 | tf_op jit(solution)/shard_map/reshape | solution.py:61
  81.8 2.8 %gather_fusion.1 = bf16[512,1024]{1,0:T(8,128)(2,1)} fusion(bf16[640,1024]{1,0:T(8,128)(2,1)S(1)} %reshape.146, s32[1024]{0:T(1024)S(1)} %pad_clamp_fusion), kind=kCustom, calls=%fused_computation.1 | custom fusion | bytes 2099200 | tf_op jit(solution)/shard_map/jit(_take)/gather | solution.py:61
  84.6 1.4 gather.15
  86.0 1.3 copy.48
  87.4 1.3 bitcast_select_fusion
  88.7 5.0 %fusion.24 = bf16[256,1024]{1,0:T(8,128)(2,1)} fusion(bf16[1024,1024]{1,0:T(8,128)(2,1)S(1)} %copy-done, bf16[2176,1024]{1,0:T(8,128)(2,1)} %param.17, bf16[256,128]{0,1:T(8,128)(2,1)S(1)} %copy.49, bf16[256,2048]{0,1:T(8,128)(2,1)S(1)} %bitcast_select_fusion, f32[256]{0:T(256)S(1)} %get-tuple-element.8, f32[1024]{0:T(1024)S(1)} %copy-done.9, ...), kind=kOutput, calls=%fused_computation.39 | convolution fusion | flops 1681522688 | bytes 8201216 | tf_op jit(solution)/shard_map/dot_general | solution.py:70
  93.7 2.5 %scatter_custom_fusion.2 = bf16[640,1024]{1,0:T(8,128)(2,1)S(1)} fusion(s32[256]{0:T(256)S(1)} %bitcast.40, bf16[256,1024]{1,0:T(8,128)(2,1)} %fusion.24, bf16[]{:T(256)} %constant.29.clone.1), kind=kCustom, calls=%fused_computation.48 | custom fusion | bytes 1311232 | tf_op jit(solution)/shard_map/scatter | solution.py:74
  96.3 1.3 reshape.147
  97.6 6.1 %all-to-all-start.3 = ((bf16[32,20,1024]{2,1,0:T(8,128)(2,1)}), bf16[32,20,1024]{2,1,0:T(8,128)(2,1)}, u32[]{:S(2)}, u32[]{:S(2)}) async-start(bf16[32,20,1024]{2,1,0:T(8,128)(2,1)} %reshape.147), calls=%async_computation.3 | async-start | bytes 3145728 | tf_op jit(solution)/shard_map/all_to_all | solution.py:77
  104.5 9.4 %fusion.43 = f32[640,3072]{1,0:T(8,128)} fusion(bf16[1024,3072]{1,0:T(8,128)(2,1)} %param.22, bf16[640,1024]{1,0:T(8,128)(2,1)S(1)} %copy-done.2, pred[640]{0:T(1024)(128)(4,1)S(1)} %compare_and_fusion.1), kind=kOutput, calls=%fused_computation.50 | convolution fusion | flops 4027187200 | bytes 15467136 | tf_op jit(solution)/shard_map/dot_general | solution.py:10
  113.9 28.5 %all-to-all-done.3 = bf16[32,20,1024]{2,1,0:T(8,128)(2,1)} async-done(((bf16[32,20,1024]{2,1,0:T(8,128)(2,1)}), bf16[32,20,1024]{2,1,0:T(8,128)(2,1)}, u32[]{:S(2)}, u32[]{:S(2)}) %all-to-all-start.3) | async-done | bytes 1310752 | tf_op jit(solution)/shard_map/all_to_all | solution.py:77
  142.4 3.3 %reshape.148 = bf16[640,1024]{1,0:T(8,128)(2,1)} reshape(bf16[32,20,1024]{2,1,0:T(8,128)(2,1)} %all-to-all-done.3) | data formatting | bytes 2621440 | tf_op jit(solution)/shard_map/reshape | solution.py:94
  145.6 11.6 %convolution_add_fusion = f32[640,3072]{1,0:T(8,128)} fusion(bf16[1024,3072]{1,0:T(8,128)(2,1)} %param.21, f32[3072]{0:T(1024)S(1)} %copy-done.8, bf16[640,1024]{1,0:T(8,128)(2,1)} %reshape.148, f32[640]{0:T(1024)S(1)} %broadcast_maximum_fusion, s32[640]{0:T(1024)S(1)} %eq.50), kind=kOutput, calls=%fused_computation.6 | convolution fusion | flops 4869079040 | bytes 15483904 | tf_op jit(solution)/shard_map/dot_general | solution.py:9
  157.3 16.4 %scatter_custom_fusion.3 = bf16[1024,1024]{1,0:T(8,128)(2,1)} fusion(bf16[1024,1024]{1,0:T(8,128)(2,1)} %copy.54, s32[640]{0:T(1024)} %copy-done.5, f32[640,3072]{1,0:T(8,128)} %fusion.43, f32[640,3072]{1,0:T(8,128)} %convolution_add_fusion, f32[]{:T(128)} %constant.31.clone.1, pred[640]{0:T(1024)(128)(4,1)S(1)} %broadcast_compare_fusion, ...), kind=kCustom, calls=%fused_computation.35 | custom fusion | flops 11796480 | bytes 19138816 | tf_op jit(solution)/shard_map/scatter | solution.py:99
  (60 shorter events, 8.6 us)
Async XLA Ops:
  0.0 88.7 %copy-start = (bf16[1024,1024]{1,0:T(8,128)(2,1)S(1)}, bf16[1024,1024]{1,0:T(8,128)(2,1)}, u32[]{:S(2)}) copy-start(bf16[1024,1024]{1,0:T(8,128)(2,1)} %param.19) | copy-start | bytes 6291460
  0.0 3.2 %copy-start.4 = (s32[256,2]{0,1:T(2,128)S(1)}, s32[256,2]{0,1:T(2,128)}, u32[]{:S(2)}) copy-start(s32[256,2]{0,1:T(2,128)} %param.13) | copy-start | bytes 6148
  0.0 5.4 %copy-start.7 = (s32[256,2]{0,1:T(2,128)S(1)}, s32[256,2]{0,1:T(2,128)}, u32[]{:S(2)}) copy-start(s32[256,2]{0,1:T(2,128)} %param.14) | copy-start | bytes 6148
  5.8 0.6 copy-start.6
  24.7 5.8 %copy-start.5 = (s32[640]{0:T(1024)}, s32[640]{0:T(1024)S(1)}, u32[]{:S(2)}) copy-start(s32[640]{0:T(1024)S(1)} %fusion.49) | copy-start | bytes 7684
  30.4 4.2 %copy-start.1 = (bf16[640,1024]{1,0:T(8,128)(2,1)}, bf16[640,1024]{1,0:T(8,128)(2,1)S(1)}, u32[]{:S(2)}) copy-start(bf16[640,1024]{1,0:T(8,128)(2,1)S(1)} %gather_fusion) | copy-start | bytes 3932164
  34.6 3.7 %copy-start.3 = (bf16[256,128]{1,0:T(8,128)(2,1)S(1)}, bf16[256,128]{1,0:T(8,128)(2,1)}, u32[]{:S(2)}) copy-start(bf16[256,128]{1,0:T(8,128)(2,1)} %param.16) | copy-start | bytes 196612
  34.6 42.4 %all-to-all-start.2 = ((bf16[32,20,1024]{2,1,0:T(8,128)(2,1)}), bf16[32,20,1024]{2,1,0:T(8,128)(2,1)}, u32[]{:S(2)}, u32[]{:S(2)}) async-start(bf16[32,20,1024]{2,1,0:T(8,128)(2,1)} %broadcast_select_fusion), calls=%async_computation.2 | async-start | bytes 3145728 | tf_op jit(solution)/shard_map/all_to_all | solution.py:54
  77.0 20.6 %all-to-all-start.1 = ((bf16[32,1,20]{2,1,0:T(2,128)(2,1)}), bf16[32,1,20]{2,1,0:T(2,128)(2,1)S(1)}, u32[]{:S(2)}, u32[]{:S(2)}) async-start(bf16[32,1,20]{2,1,0:T(2,128)(2,1)} %all_to_all.24), calls=%async_computation.1 | async-start | bytes 32768 | tf_op jit(solution)/shard_map/all_to_all | solution.py:84
  86.0 2.7 %copy-start.9 = (f32[1024]{0:T(1024)S(1)}, f32[1024]{0:T(1024)}, u32[]{:S(2)}) copy-start(f32[1024]{0:T(1024)} %param.20) | copy-start | bytes 12292
  86.0 2.7 %copy-start.10 = (f32[1024]{0:T(1024)S(1)}, f32[1024]{0:T(1024)}, u32[]{:S(2)}) copy-start(f32[1024]{0:T(1024)} %param.18) | copy-start | bytes 12292
  97.6 6.9 %copy-start.2 = (bf16[640,1024]{1,0:T(8,128)(2,1)S(1)}, bf16[640,1024]{1,0:T(8,128)(2,1)}, u32[]{:S(2)}) copy-start(bf16[640,1024]{1,0:T(8,128)(2,1)} %copy-done.1) | copy-start | bytes 3932164
  97.6 44.8 %all-to-all-start.3 = ((bf16[32,20,1024]{2,1,0:T(8,128)(2,1)}), bf16[32,20,1024]{2,1,0:T(8,128)(2,1)}, u32[]{:S(2)}, u32[]{:S(2)}) async-start(bf16[32,20,1024]{2,1,0:T(8,128)(2,1)} %reshape.147), calls=%async_computation.3 | async-start | bytes 3145728 | tf_op jit(solution)/shard_map/all_to_all | solution.py:77
  113.9 31.7 %copy-start.8 = (f32[3072]{0:T(1024)S(1)}, f32[3072]{0:T(1024)}, u32[]{:S(2)}) copy-start(f32[3072]{0:T(1024)} %param.23) | copy-start | bytes 36868
where the time goes:
time: 174 us
  waiting for transfers between devices  61.9 us (36%)
  local copies, waits for them, and re-layouts  33.8 us (19%)
  matrix products  26.5 us (15%)
  other arithmetic  24.8 us (14%)
  blocking collectives  14.2 us (8%)
  starting transfers between devices  12.2 us (7%)
    all_to_all x1, waiting for transfers between devices, on_device(): lax.all_to_all(answers.reshape(devices, capacity, feature_width), ('node'...  33.4 us
    all_to_all x1, waiting for transfers between devices, on_device(): lax.all_to_all(outgoing.reshape(devices, capacity, feature_width), ('node...  28.5 us
    scatter x1, other arithmetic, on_device(): return memory.at[flat_ids].set(renewed)  16.4 us
    all_to_all x1, blocking collectives, on_device(): lax.all_to_all(requests, ('node', 'tm'), split_axis=0, concat_axis=0, til...  14.2 us
    dot_general x1, matrix products, memory_update(): jnp.dot(aggregate, gru_in, preferred_element_type=jnp.float32) + gru_bias  11.6 us
    dot_general x1, matrix products, memory_update(): gates_hid = jnp.dot(memory, gru_hid, preferred_element_type=jnp.float32)  9.38 us
    gather x2, local copies, waits for them, and re-layouts, on_device(): answers = jnp.take(memory, flat_ids, axis=0)  7.15 us
    all_to_all x1, starting transfers between devices, on_device(): lax.all_to_all(outgoing.reshape(devices, capacity, feature_width), ('node...  6.13 us
  transfers between devices with their start and end apart: 3, of which 2 were waited for; matrix products, arithmetic and copies ran while one was open for 19% of the time, Pallas kernels for 0%

commit v1 on v0

v1 whole, which is shorter than its diff:
```python
import functools

import jax
import jax.numpy as jnp
from jax import lax
from jax.experimental import pallas as pl
from jax.experimental.pallas import tpu as pltpu
from jax.sharding import PartitionSpec as P

BF = jnp.bfloat16
F32 = jnp.float32
I32 = jnp.int32
QUARTERS = 4
FIELDS = 8
TILE = 256


def div(x, n):
    if n & (n - 1) == 0:
        return lax.shift_right_logical(x, jnp.full_like(x, n.bit_length() - 1))
    return lax.div(x, jnp.full_like(x, n))


def rem(x, n):
    if n & (n - 1) == 0:
        return lax.bitwise_and(x, jnp.full_like(x, n - 1))
    return lax.rem(x, jnp.full_like(x, n))


def iota(rows, columns, axis):
    return lax.broadcasted_iota(I32, (rows, columns), axis)


def ones_where(condition):
    return jnp.where(condition, 1.0, 0.0).astype(BF)


def dot(a, b):
    return jnp.dot(a, b, preferred_element_type=F32)


def to_column(row):
    n = row.shape[1]
    return jnp.sum(jnp.where(iota(n, n, 0) == iota(n, n, 1), row, 0.0), axis=1, keepdims=True)


def to_row(column):
    n = column.shape[0]
    return jnp.sum(jnp.where(iota(n, n, 0) == iota(n, n, 1), column, 0.0), axis=0, keepdims=True)


def kernel(
    cfg,
    owner_ref, row_ref, mask_ref, feat_ref, b1_ref, b2_ref, gb_ref,
    mem_hbm, w1_hbm, w2_hbm, wi_hbm, wh_hbm,
    out_ref,
    mem, w1, w2, wi, wh, gh, table_out, table_in, fetched, hidden, tally, agg,
    main_row, main_flag, tail_row, tail_flag, tail_acc,
    ans_main, ret_main, msg_main, inc_main, ans_tail, ret_tail, msg_tail, inc_tail,
    load_sem, send_sem, recv_sem, own_sem,
):
    D, tm, m, R = cfg
    N, DM = mem.shape
    E = owner_ref.shape[1]
    HID = hidden.shape[1]
    QW = DM // QUARTERS
    tr = QUARTERS * R
    me = lax.axis_index("node") * tm + lax.axis_index("tm")

    loads = []
    for i, (src, dst) in enumerate(
        ((mem_hbm, mem), (wh_hbm, wh), (w1_hbm, w1), (w2_hbm, w2), (wi_hbm, wi))
    ):
        c = pltpu.make_async_copy(src, dst, load_sem.at[i])
        c.start()
        loads.append(c)

    barrier = pltpu.get_barrier_semaphore()

    @pl.loop(1, D)
    def _(i):
        peer = lax.rem(me + i, D)
        pl.semaphore_signal(
            barrier, inc=1, device_id=(peer // tm, lax.rem(peer, tm)),
            device_id_type=pl.DeviceIdType.MESH,
        )

    def start_exchange(k, pieces):
        for n, (src, dst, rows) in enumerate(pieces):
            pltpu.make_async_copy(
                src.at[pl.ds(pl.multiple_of(me * rows, rows), rows)],
                dst.at[pl.ds(pl.multiple_of(me * rows, rows), rows)],
                own_sem.at[k + n],
            ).start()

        @pl.loop(1, D)
        def _(i):
            peer = lax.rem(me + i, D)
            for n, (src, dst, rows) in enumerate(pieces):
                pltpu.make_async_remote_copy(
                    src_ref=src.at[pl.ds(pl.multiple_of(peer * rows, rows), rows)],
                    dst_ref=dst.at[pl.ds(pl.multiple_of(me * rows, rows), rows)],
                    send_sem=send_sem.at[k + n],
                    recv_sem=recv_sem.at[k + n],
                    device_id=(peer // tm, lax.rem(peer, tm)),
                    device_id_type=pl.DeviceIdType.MESH,
                ).start()

    def wait_received(k, pieces):
        for n, (src, dst, rows) in enumerate(pieces):
            part = dst.at[pl.ds(0, (D - 1) * rows)]
            pltpu.make_async_copy(part, part, recv_sem.at[k + n]).wait()
            own = dst.at[pl.ds(0, rows)]
            pltpu.make_async_copy(own, own, own_sem.at[k + n]).wait()

    def wait_sent(k, pieces):
        for n, (src, dst, rows) in enumerate(pieces):
            part = src.at[pl.ds(0, (D - 1) * rows)]
            pltpu.make_async_copy(part, part, send_sem.at[k + n]).wait()

    tables = [(table_out, table_in, FIELDS)]
    answers = [(ans_tail, ret_tail, tr)]
    messages = [(msg_tail, inc_tail, tr)]
    if m:
        answers.append((ans_main, ret_main, m))
        messages.append((msg_main, inc_main, m))

    owner = jnp.concatenate([owner_ref[0:1, :], owner_ref[1:2, :]], axis=1)
    wanted = jnp.concatenate([row_ref[0:1, :], row_ref[1:2, :]], axis=1)
    flag = jnp.concatenate([jnp.zeros((1, E), I32), mask_ref[...]], axis=1)
    onehot = jnp.where(iota(D, 2 * E, 0) == owner, 1.0, 0.0)
    earlier = ones_where(iota(2 * E, 2 * E, 0) < iota(2 * E, 2 * E, 1))
    position = jnp.sum(onehot * dot(onehot.astype(BF), earlier), axis=0, keepdims=True).astype(I32)
    field = rem(iota(D * FIELDS, 2 * E, 0), FIELDS)
    value = jnp.where(
        field == 0, div(wanted, 32) + 1,
        jnp.where(field == 1, rem(wanted, 32), jnp.where(field == 2, flag, 0)),
    )
    value = jnp.where(div(iota(D * FIELDS, 2 * E, 0), FIELDS) == owner, value, 0)
    place = ones_where(iota(128, 2 * E, 0) == position)
    table_out[...] = lax.dot_general(
        value.astype(F32).astype(BF), place, (((1,), (1,)), ((), ())), preferred_element_type=F32
    )
    pl.semaphore_wait(barrier, D - 1)
    start_exchange(0, tables)

    far = -4 * D * (m + tr)
    at_main = jnp.where(position < m, owner * m + position, far)
    at_tail = jnp.where(position >= m, owner * tr + position - m, far)
    main_column = to_column(at_main.astype(F32)).astype(I32)
    tail_column = to_column(at_tail.astype(F32)).astype(I32)
    sent_main = jnp.where(flag[:, E:] > 0, at_main[:, E:], far)
    sent_tail = jnp.where(flag[:, E:] > 0, at_tail[:, E:], far)

    loads[0].wait()
    wait_received(0, tables)

    table = table_in[...].astype(BF)

    def slots(base, size, block, first, period):
        s = base + iota(size, D * FIELDS, 0)
        field_row = iota(size, D * FIELDS, 1)
        start = div(s, block) * FIELDS
        pick = jnp.where(field_row == start, 32.0, jnp.where(field_row == start + 1, 1.0, 0.0))
        lane = iota(size, 128, 1) == first + rem(base + iota(size, 128, 0), period)
        ids = jnp.sum(jnp.where(lane, dot(pick.astype(BF), table), 0.0), axis=1, keepdims=True)
        marks = jnp.sum(
            jnp.where(lane, dot(ones_where(field_row == start + 2), table), 0.0),
            axis=1, keepdims=True,
        )
        return ids - 32.0, marks

    chunk = min(512, D * tr)

    @pl.loop(0, D * tr // chunk)
    def _(step):
        base = pl.multiple_of(step * chunk, chunk)
        ids, marks = slots(base, chunk, tr, m, R)
        quarter = rem(div(base + iota(chunk, 1, 0), R), QUARTERS)
        tail_row[:, pl.ds(base, chunk)] = to_row(ids).astype(I32)
        tail_flag[:, pl.ds(base, chunk)] = to_row(jnp.where(quarter == 0, marks, 0.0))
        total = jnp.zeros((chunk, QW), F32)
        nodes = iota(chunk, N, 1)
        for q in range(QUARTERS):
            hit = ones_where(nodes == jnp.where(quarter == q, ids.astype(I32), -1))
            total = total + dot(hit, mem[:, q * QW : (q + 1) * QW])
        ans_tail[pl.ds(base, chunk), :] = total.astype(BF)

    if m:
        main_chunk = min(512, D * m)

        @pl.loop(0, D * m // main_chunk)
        def _(step):
            base = pl.multiple_of(step * main_chunk, main_chunk)
            ids, marks = slots(base, main_chunk, m, 0, m)
            main_row[:, pl.ds(base, main_chunk)] = to_row(ids).astype(I32)
            main_flag[:, pl.ds(base, main_chunk)] = to_row(marks)
            hit = ones_where(iota(main_chunk, N, 1) == ids.astype(I32))

            @pl.loop(0, QUARTERS)
            def _(q):
                cols = pl.ds(pl.multiple_of(q * QW, QW), QW)
                ans_main[pl.ds(base, main_chunk), cols] = dot(hit, mem[:, cols]).astype(BF)

    start_exchange(1, answers)

    loads[1].wait()

    @pl.loop(0, 3 * DM // TILE)
    def _(t):
        cols = pl.ds(pl.multiple_of(t * TILE, TILE), TILE)
        gh[:, cols] = dot(mem[...], wh[:, cols])

    @pl.loop(0, N // TILE)
    def _(t):
        base = pl.multiple_of(t * TILE, TILE)
        nodes = base + iota(TILE, D * tr, 0)
        count = jnp.sum(jnp.where(tail_row[...] == nodes, tail_flag[...], 0.0), axis=1, keepdims=True)
        if m:
            nodes = base + iota(TILE, D * m, 0)
            count = count + jnp.sum(
                jnp.where(main_row[...] == nodes, main_flag[...], 0.0), axis=1, keepdims=True
            )
        tally[pl.ds(base, TILE), :] = count

    loads[2].wait()
    loads[3].wait()
    wait_received(1, answers)

    if m:
        from_main = ones_where(iota(2 * E, D * m, 1) == main_column)

    @pl.loop(0, QUARTERS)
    def _(q):
        cols = pl.ds(pl.multiple_of(q * QW, QW), QW)
        got = dot(ones_where(iota(2 * E, D * tr, 1) == tail_column + q * R), ret_tail[...])
        if m:
            got = got + dot(from_main, ret_main[:, cols])
        fetched[:, cols] = got.astype(BF)

    @pl.loop(0, HID // TILE)
    def _(t):
        cols = pl.ds(pl.multiple_of(t * TILE, TILE), TILE)
        h = dot(fetched[0:E, :], w1[0:DM, cols]) + dot(fetched[E : 2 * E, :], w1[DM : 2 * DM, cols])
        h = h + dot(feat_ref[...], w1[2 * DM :, cols]) + b1_ref[:, cols]
        hidden[:, cols] = jnp.maximum(h, 0.0).astype(BF)

    tail_acc[...] = jnp.zeros_like(tail_acc)
    if m:
        to_main = ones_where(iota(D * m, E, 0) == sent_main)

    @pl.loop(0, QUARTERS)
    def _(q):
        cols = pl.ds(pl.multiple_of(q * QW, QW), QW)
        message = (dot(hidden[...], w2[:, cols]) + b2_ref[:, cols]).astype(BF)
        if m:
            msg_main[:, cols] = dot(to_main, message).astype(BF)
        tail_acc[...] += dot(ones_where(iota(D * tr, E, 0) == sent_tail + q * R), message)

    msg_tail[...] = tail_acc[...].astype(BF)
    k = 1 + len(answers)
    start_exchange(k, messages)
    wait_sent(0, tables)
    wait_sent(1, answers)
    loads[4].wait()
    wait_received(k, messages)

    @pl.loop(0, N // TILE)
    def _(t):
        base = pl.multiple_of(t * TILE, TILE)
        rows = pl.ds(base, TILE)
        count = tally[rows, :]
        nodes = base + iota(TILE, D * tr, 0)
        quarter = rem(div(iota(1, D * tr, 1), R), QUARTERS)
        if m:
            hit_main = ones_where(main_row[...] == base + iota(TILE, D * m, 0))

        @pl.loop(0, QUARTERS)
        def _(q):
            cols = pl.ds(pl.multiple_of(q * QW, QW), QW)
            hit = ones_where(jnp.where(quarter == q, tail_row[...], -1) == nodes)
            summed = dot(hit, inc_tail[...])
            if m:
                summed = summed + dot(hit_main, inc_main[:, cols])
            agg[:, cols] = (summed / jnp.maximum(count, 1.0)).astype(BF)

        @pl.loop(0, DM // TILE)
        def _(c):
            def part(g):
                cols = pl.ds(pl.multiple_of(g * DM + c * TILE, TILE), TILE)
                return dot(agg[...], wi[:, cols]) + gb_ref[:, cols], gh[rows, cols]

            cols = pl.ds(pl.multiple_of(c * TILE, TILE), TILE)
            gi_r, gh_r = part(0)
            gi_z, gh_z = part(1)
            gi_c, gh_c = part(2)
            reset = 0.5 * jnp.tanh(0.5 * (gi_r + gh_r)) + 0.5
            update = 0.5 * jnp.tanh(0.5 * (gi_z + gh_z)) + 0.5
            candidate = jnp.tanh(gi_c + reset * gh_c)
            previous = mem[rows, cols].astype(F32)
            renewed = (1.0 - update) * candidate + update * previous
            out_ref[rows, cols] = jnp.where(count > 0.5, renewed, previous).astype(BF)

    wait_sent(k, messages)


def on_device(
    mesh_sizes,
    memory,
    ends_owner,
    ends_row,
    event_mask,
    edge_feat,
    msg_w1,
    msg_b1,
    msg_w2,
    msg_b2,
    gru_in,
    gru_hid,
    gru_bias,
):
    D, tm = mesh_sizes
    E = ends_owner.shape[0]
    N, DM = memory.shape
    HID = msg_w2.shape[0]
    cap = 5 * E // (2 * D)
    m = cap // 16 * 16
    R = max(4, -(-(cap - m) // 4) * 4)
    tr = QUARTERS * R
    QW = DM // QUARTERS
    mains = max(m, 1) * D if m else 16
    vmem = pl.BlockSpec(memory_space=pltpu.VMEM)
    anywhere = pl.BlockSpec(memory_space=pl.ANY)
    return pl.pallas_call(
        functools.partial(kernel, (D, tm, m, R)),
        out_shape=jax.ShapeDtypeStruct((N, DM), BF),
        in_specs=[vmem] * 7 + [anywhere] * 5,
        out_specs=vmem,
        scratch_shapes=[
            pltpu.VMEM(memory.shape, BF),
            pltpu.VMEM(msg_w1.shape, BF),
            pltpu.VMEM(msg_w2.shape, BF),
            pltpu.VMEM(gru_in.shape, BF),
            pltpu.VMEM(gru_hid.shape, BF),
            pltpu.VMEM((N, 3 * DM), F32),
            pltpu.VMEM((D * FIELDS, 128), F32),
            pltpu.VMEM((D * FIELDS, 128), F32),
            pltpu.VMEM((2 * E, DM), BF),
            pltpu.VMEM((E, HID), BF),
            pltpu.VMEM((N, 1), F32),
            pltpu.VMEM((TILE, DM), BF),
            pltpu.VMEM((1, mains), I32),
            pltpu.VMEM((1, mains), F32),
            pltpu.VMEM((1, D * tr), I32),
            pltpu.VMEM((1, D * tr), F32),
            pltpu.VMEM((D * tr, QW), F32),
        ]
        + [pltpu.VMEM((mains, DM), BF)] * 4
        + [pltpu.VMEM((D * tr, QW), BF)] * 4
        + [
            pltpu.SemaphoreType.DMA((5,)),
            pltpu.SemaphoreType.DMA((5,)),
            pltpu.SemaphoreType.DMA((5,)),
            pltpu.SemaphoreType.DMA((5,)),
        ],
        compiler_params=pltpu.CompilerParams(
            collective_id=0, has_side_effects=True, vmem_limit_bytes=60 * 2**20
        ),
    )(
        ends_owner.T,
        ends_row.T,
        event_mask.reshape(1, E),
        edge_feat,
        msg_b1.reshape(1, -1),
        msg_b2.reshape(1, -1),
        gru_bias.reshape(1, -1),
        memory,
        msg_w1,
        msg_w2,
        gru_in,
        gru_hid,
    )


def solution(mesh):
    sizes = (mesh.shape["node"] * mesh.shape["tm"], mesh.shape["tm"])
    split = P(("node", "tm"))
    return jax.shard_map(
        functools.partial(on_device, sizes),
        mesh=mesh,
        in_specs=(split,) * 5 + (P(),) * 7,
        out_specs=split,
        check_vma=False,
    )
```

time: 174 us -> 103 us (0.59)
  the two profiles are of different devices: /device:TPU:0 before, /device:TPU:25 now
where the time goes in v1:
time: 103 us; the launch traced here: 102 us
  Pallas kernels  99.4 us (97%)
  local copies, waits for them, and re-layouts  3.08 us (3%)
    pallas_call x1, Pallas kernels, on_device(): pl.pallas_call(functools.partial(kernel, (D, tm, m, R)), out_shape=jax.Sh...  99.4 us
    unnamed x1, local copies, waits for them, and re-layouts  3.08 us

profile of v1, /device:TPU:25, one launch (start us, length us, event | category | flops | bytes accessed | tf_op | source)
XLA Modules:
  0.0 102.5 jit_solution(11352542222016889074)
XLA Ops:
  0.0 99.4 %shard_map.118 = bf16[1024,1024]{1,0:T(8,128)(2,1)} custom-call(s32[2,256]{1,0:T(2,128)} %bitcast.9, s32[2,256]{1,0:T(2,128)} %bitcast.10, s32[1,256]{1,0:T(1,128)} %bitcast.11, bf16[256,128]{1,0:T(8,128)(2,1)} %feat_ref.1, f32[1,1024]{1,0:T(1,128)} %bitcast.7, f32[1,1024]{1,0:T(1,128)} %bitcast.8, f32[1,3072]{1,0:T(1,128)} %bitcast.6, ...), custom_call_target="tpu_custom_call" | custom-call | tf_op jit(solution)/shard_map/pallas_call | solution.py:334
  99.4 3.1 %copy.14 = bf16[1024,1024]{1,0:T(8,128)(2,1)} copy(bf16[1024,1024]{1,0:T(8,128)(2,1)} %shard_map.118) | data formatting | bytes 4194304

commit v2 on v1

--- a/solution.py
+++ b/solution.py
@@ -13,6 +13,7 @@
 QUARTERS = 4
 FIELDS = 8
 TILE = 256
+HALVES = 2
 
 
 def div(x, n):
@@ -51,25 +52,27 @@
 
 def kernel(
     cfg,
-    owner_ref, row_ref, mask_ref, feat_ref, b1_ref, b2_ref, gb_ref,
-    mem_hbm, w1_hbm, w2_hbm, wi_hbm, wh_hbm,
-    out_ref,
-    mem, w1, w2, wi, wh, gh, table_out, table_in, fetched, hidden, tally, agg,
-    main_row, main_flag, tail_row, tail_flag, tail_acc,
+    owner_ref, row_ref, mask_ref, feat_ref, b1_ref, b2_ref,
+    mem_hbm, w1_hbm, w2_hbm, wh_hbm,
+    agg_out, gh_out, held_out, rank_out, total_out,
+    mem, w1, w2, wh, gh, held, table_out, table_in, fetched, acc, hidden, tally,
+    main_row, main_flag, tail_row, tail_flag, tail_acc, sums,
     ans_main, ret_main, msg_main, inc_main, ans_tail, ret_tail, msg_tail, inc_tail,
-    load_sem, send_sem, recv_sem, own_sem,
+    load_sem, send_sem, recv_sem, own_sem, store_sem,
 ):
     D, tm, m, R = cfg
     N, DM = mem.shape
     E = owner_ref.shape[1]
     HID = hidden.shape[1]
     QW = DM // QUARTERS
+    HW = DM // HALVES
     tr = QUARTERS * R
+    ranks = agg_out.shape[0]
     me = lax.axis_index("node") * tm + lax.axis_index("tm")
 
     loads = []
     for i, (src, dst) in enumerate(
-        ((mem_hbm, mem), (wh_hbm, wh), (w1_hbm, w1), (w2_hbm, w2), (wi_hbm, wi))
+        ((mem_hbm, mem), (wh_hbm, wh), (w1_hbm, w1), (w2_hbm, w2))
     ):
         c = pltpu.make_async_copy(src, dst, load_sem.at[i])
         c.start()
@@ -119,11 +122,10 @@
             pltpu.make_async_copy(part, part, send_sem.at[k + n]).wait()
 
     tables = [(table_out, table_in, FIELDS)]
-    answers = [(ans_tail, ret_tail, tr)]
-    messages = [(msg_tail, inc_tail, tr)]
-    if m:
-        answers.append((ans_main, ret_main, m))
-        messages.append((msg_main, inc_main, m))
+    ans_t = [(ans_tail, ret_tail, tr)]
+    msg_t = [(msg_tail, inc_tail, tr)]
+    ans_m = [[(ans_main.at[h], ret_main.at[h], m)] if m else [] for h in range(HALVES)]
+    msg_m = [[(msg_main.at[h], inc_main.at[h], m)] if m else [] for h in range(HALVES)]
 
     owner = jnp.concatenate([owner_ref[0:1, :], owner_ref[1:2, :]], axis=1)
     wanted = jnp.concatenate([row_ref[0:1, :], row_ref[1:2, :]], axis=1)
@@ -186,30 +188,26 @@
             total = total + dot(hit, mem[:, q * QW : (q + 1) * QW])
         ans_tail[pl.ds(base, chunk), :] = total.astype(BF)
 
+    start_exchange(1, ans_t)
+
     if m:
         main_chunk = min(512, D * m)
-
-        @pl.loop(0, D * m // main_chunk)
-        def _(step):
-            base = pl.multiple_of(step * main_chunk, main_chunk)
-            ids, marks = slots(base, main_chunk, m, 0, m)
-            main_row[:, pl.ds(base, main_chunk)] = to_row(ids).astype(I32)
-            main_flag[:, pl.ds(base, main_chunk)] = to_row(marks)
-            hit = ones_where(iota(main_chunk, N, 1) == ids.astype(I32))
-
-            @pl.loop(0, QUARTERS)
-            def _(q):
-                cols = pl.ds(pl.multiple_of(q * QW, QW), QW)
-                ans_main[pl.ds(base, main_chunk), cols] = dot(hit, mem[:, cols]).astype(BF)
-
-    start_exchange(1, answers)
-
-    loads[1].wait()
-
-    @pl.loop(0, 3 * DM // TILE)
-    def _(t):
-        cols = pl.ds(pl.multiple_of(t * TILE, TILE), TILE)
-        gh[:, cols] = dot(mem[...], wh[:, cols])
+        main_steps = D * m // main_chunk
+        for h in range(HALVES):
+
+            @pl.loop(0, main_steps)
+            def _(step):
+                base = pl.multiple_of(step * main_chunk, main_chunk)
+                ids, marks = slots(base, main_chunk, m, 0, m)
+                if h == 0:
+                    main_row[:, pl.ds(base, main_chunk)] = to_row(ids).astype(I32)
+                    main_flag[:, pl.ds(base, main_chunk)] = to_row(marks)
+                hit = ones_where(iota(main_chunk, N, 1) == ids.astype(I32))
+                ans_main[h, pl.ds(base, main_chunk), :] = dot(
+                    hit, mem[:, h * HW : (h + 1) * HW]
+                ).astype(BF)
+
+            start_exchange(2 + h, ans_m[h])
 
     @pl.loop(0, N // TILE)
     def _(t):
@@ -223,85 +221,225 @@
             )
         tally[pl.ds(base, TILE), :] = count
 
+    tally_row = to_row(tally[...])
+    touched_row = jnp.where(tally_row > 0.5, 1.0, 0.0)
+    earlier = ones_where(iota(N, N, 0) < iota(N, N, 1))
+    before = dot(jnp.broadcast_to(touched_row, (8, N)).astype(BF), earlier)[0:1, :]
+    rank_row = jnp.where(touched_row > 0.5, before, -1.0)
+    rank_column = to_column(rank_row)
+    rank_out[...] = jnp.broadcast_to(rank_column, (N, 128)).astype(I32)
+    total_out[...] = jnp.broadcast_to(
+        jnp.sum(touched_row, axis=1, keepdims=True), (8, 128)
+    ).astype(I32)
+
+    def rank_slots(row_ref, count, size):
+        @pl.loop(0, count // size)
+        def _(step):
+            cols = pl.ds(pl.multiple_of(step * size, size), size)
+            same = iota(N, size, 0) == row_ref[:, cols]
+            row_ref[:, cols] = jnp.sum(
+                jnp.where(same, rank_column, 0.0), axis=0, keepdims=True
+            ).astype(I32)
+
+    rank_slots(tail_row, D * tr, chunk)
+    if m:
+        rank_slots(main_row, D * m, main_chunk)
+
+    loads[1].wait()
+
+    @pl.loop(0, ranks // TILE)
+    def _(t):
+        base = pl.multiple_of(t * TILE, TILE)
+        rows = pl.ds(base, TILE)
+        pick = rank_row.astype(I32) == base + iota(TILE, N, 0)
+        tally[rows, :] = jnp.sum(jnp.where(pick, tally_row, 0.0), axis=1, keepdims=True)
+        pick = ones_where(pick)
+
+        @pl.loop(0, DM // TILE)
+        def _(c):
+            cols = pl.ds(pl.multiple_of(c * TILE, TILE), TILE)
+            held[rows, cols] = dot(pick, mem[:, cols]).astype(BF)
+
+    @pl.loop(0, 3 * DM // TILE)
+    def _(t):
+        cols = pl.ds(pl.multiple_of(t * TILE, TILE), TILE)
+        gh[:, cols] = dot(held[...], wh[:, cols])
+
+    stores = [
+        pltpu.make_async_copy(gh, gh_out, store_sem.at[0]),
+        pltpu.make_async_copy(held, held_out, store_sem.at[1]),
+    ]
+    for c in stores:
+        c.start()
+
     loads[2].wait()
     loads[3].wait()
-    wait_received(1, answers)
-
-    if m:
-        from_main = ones_where(iota(2 * E, D * m, 1) == main_column)
-
-    @pl.loop(0, QUARTERS)
-    def _(q):
-        cols = pl.ds(pl.multiple_of(q * QW, QW), QW)
-        got = dot(ones_where(iota(2 * E, D * tr, 1) == tail_column + q * R), ret_tail[...])
-        if m:
-            got = got + dot(from_main, ret_main[:, cols])
-        fetched[:, cols] = got.astype(BF)
+    feat_width = feat_ref.shape[1]
 
     @pl.loop(0, HID // TILE)
     def _(t):
         cols = pl.ds(pl.multiple_of(t * TILE, TILE), TILE)
-        h = dot(fetched[0:E, :], w1[0:DM, cols]) + dot(fetched[E : 2 * E, :], w1[DM : 2 * DM, cols])
-        h = h + dot(feat_ref[...], w1[2 * DM :, cols]) + b1_ref[:, cols]
-        hidden[:, cols] = jnp.maximum(h, 0.0).astype(BF)
+        acc[:, cols] = dot(feat_ref[...], w1[2 * DM : 2 * DM + feat_width, cols]) + b1_ref[:, cols]
+
+    wait_received(1, ans_t)
+    if m:
+        from_main = ones_where(iota(2 * E, D * m, 1) == main_column)
+
+    for h in range(HALVES):
+        wait_received(2 + h, ans_m[h])
+        got = []
+        for q in range(h * QUARTERS // HALVES, (h + 1) * QUARTERS // HALVES):
+            got.append(dot(ones_where(iota(2 * E, D * tr, 1) == tail_column + q * R), ret_tail[...]))
+        got = jnp.concatenate(got, axis=1)
+        if m:
+            got = got + dot(from_main, ret_main[h])
+        fetched[...] = got.astype(BF)
+
+        @pl.loop(0, HID // TILE)
+        def _(t):
+            cols = pl.ds(pl.multiple_of(t * TILE, TILE), TILE)
+            total = acc[:, cols] + dot(fetched[0:E, :], w1[h * HW : (h + 1) * HW, cols])
+            total = total + dot(fetched[E : 2 * E, :], w1[DM + h * HW : DM + (h + 1) * HW, cols])
+            if h == HALVES - 1:
+                hidden[:, cols] = jnp.maximum(total, 0.0).astype(BF)
+            else:
+                acc[:, cols] = total
 
     tail_acc[...] = jnp.zeros_like(tail_acc)
     if m:
         to_main = ones_where(iota(D * m, E, 0) == sent_main)
-
-    @pl.loop(0, QUARTERS)
-    def _(q):
-        cols = pl.ds(pl.multiple_of(q * QW, QW), QW)
+    k = 2 + HALVES
+    for h in range(HALVES):
+        cols = slice(h * HW, (h + 1) * HW)
         message = (dot(hidden[...], w2[:, cols]) + b2_ref[:, cols]).astype(BF)
         if m:
-            msg_main[:, cols] = dot(to_main, message).astype(BF)
-        tail_acc[...] += dot(ones_where(iota(D * tr, E, 0) == sent_tail + q * R), message)
+            msg_main[h] = dot(to_main, message).astype(BF)
+            start_exchange(k + 1 + h, msg_m[h])
+        for j in range(QUARTERS // HALVES):
+            q = h * QUARTERS // HALVES + j
+            tail_acc[...] += dot(
+                ones_where(iota(D * tr, E, 0) == sent_tail + q * R),
+                message[:, j * QW : (j + 1) * QW],
+            )
 
     msg_tail[...] = tail_acc[...].astype(BF)
-    k = 1 + len(answers)
-    start_exchange(k, messages)
+    start_exchange(k, msg_t)
     wait_sent(0, tables)
-    wait_sent(1, answers)
-    loads[4].wait()
-    wait_received(k, messages)
-
-    @pl.loop(0, N // TILE)
+    wait_sent(1, ans_t)
+    for h in range(HALVES):
+        wait_sent(2 + h, ans_m[h])
+    for c in stores:
+        c.wait()
+
+    quarter = rem(div(iota(1, D * tr, 1), R), QUARTERS)
+    for h in range(HALVES):
+        wait_received(k + 1 + h, msg_m[h])
+        if h == HALVES - 1:
+            wait_received(k, msg_t)
+        if m:
+
+            @pl.loop(0, ranks // TILE)
+            def _(t):
+                base = pl.multiple_of(t * TILE, TILE)
+                rows = pl.ds(base, TILE)
+                hit = ones_where(main_row[...] == base + iota(TILE, D * m, 0))
+                sums[rows, h * HW : (h + 1) * HW] = dot(hit, inc_main[h])
+
+    @pl.loop(0, ranks // TILE)
     def _(t):
         base = pl.multiple_of(t * TILE, TILE)
         rows = pl.ds(base, TILE)
-        count = tally[rows, :]
-        nodes = base + iota(TILE, D * tr, 0)
-        quarter = rem(div(iota(1, D * tr, 1), R), QUARTERS)
-        if m:
-            hit_main = ones_where(main_row[...] == base + iota(TILE, D * m, 0))
-
-        @pl.loop(0, QUARTERS)
-        def _(q):
-            cols = pl.ds(pl.multiple_of(q * QW, QW), QW)
-            hit = ones_where(jnp.where(quarter == q, tail_row[...], -1) == nodes)
+        count = jnp.maximum(tally[rows, :], 1.0)
+        for q in range(QUARTERS):
+            cols = slice(q * QW, (q + 1) * QW)
+            wanted_rank = base + iota(TILE, D * tr, 0)
+            hit = ones_where(jnp.where(quarter == q, tail_row[...], -1) == wanted_rank)
             summed = dot(hit, inc_tail[...])
             if m:
-                summed = summed + dot(hit_main, inc_main[:, cols])
-            agg[:, cols] = (summed / jnp.maximum(count, 1.0)).astype(BF)
-
-        @pl.loop(0, DM // TILE)
+                summed = summed + sums[rows, cols]
+            agg_out[rows, cols] = (summed / count).astype(BF)
+
+    wait_sent(k, msg_t)
+    for h in range(HALVES):
+        wait_sent(k + 1 + h, msg_m[h])
+
+
+def gru_kernel(
+    total_ref, rank_ref, gb_ref, mem_ref, agg_hbm, gh_hbm, held_hbm, wi_hbm,
+    out_ref,
+    agg, gh, held, wi, fresh, load_sem, weight_sem,
+):
+    N, DM = mem_ref.shape
+    steps = DM // TILE
+    tiles = lax.div(total_ref[0, 0] + (TILE - 1), TILE)
+
+    def tile_copies(t):
+        rows = pl.ds(pl.multiple_of(t * TILE, TILE), TILE)
+        return [
+            pltpu.make_async_copy(agg_hbm.at[rows], agg, load_sem.at[0]),
+            pltpu.make_async_copy(gh_hbm.at[rows], gh, load_sem.at[1]),
+            pltpu.make_async_copy(held_hbm.at[rows], held, load_sem.at[2]),
+        ]
+
+    def weight_copies(c):
+        copies = []
+        for g in range(3):
+            cols = pl.ds(g * DM + c * TILE, TILE)
+            copies.append(
+                pltpu.make_async_copy(wi_hbm.at[:, cols], wi.at[:, cols], weight_sem.at[c, g])
+            )
+        return copies
+
+    for c in tile_copies(0):
+        c.start()
+    for c in range(steps):
+        for copy in weight_copies(c):
+            copy.start()
+    out_ref[...] = mem_ref[...]
+    for c in tile_copies(0):
+        c.wait()
+
+    def one_step(c):
+        def part(g):
+            cols = slice(g * DM + c * TILE, g * DM + (c + 1) * TILE)
+            return dot(agg[...], wi[:, cols]) + gb_ref[:, cols], gh[:, cols]
+
+        cols = slice(c * TILE, (c + 1) * TILE)
+        gi_r, gh_r = part(0)
+        gi_z, gh_z = part(1)
+        gi_c, gh_c = part(2)
+        reset = 0.5 * jnp.tanh(0.5 * (gi_r + gh_r)) + 0.5
+        update = 0.5 * jnp.tanh(0.5 * (gi_z + gh_z)) + 0.5
+        candidate = jnp.tanh(gi_c + reset * gh_c)
+        previous = held[:, cols].astype(F32)
+        fresh[:, cols] = ((1.0 - update) * candidate + update * previous).astype(BF)
+
+    def spread(base):
+        column = rank_ref[:, 0:1] - base
+        place = ones_where(column == iota(N, TILE, 1))
+        mine = (column >= 0) & (column < TILE)
+
+        @pl.loop(0, steps)
         def _(c):
-            def part(g):
-                cols = pl.ds(pl.multiple_of(g * DM + c * TILE, TILE), TILE)
-                return dot(agg[...], wi[:, cols]) + gb_ref[:, cols], gh[rows, cols]
-
             cols = pl.ds(pl.multiple_of(c * TILE, TILE), TILE)
-            gi_r, gh_r = part(0)
-            gi_z, gh_z = part(1)
-            gi_c, gh_c = part(2)
-            reset = 0.5 * jnp.tanh(0.5 * (gi_r + gh_r)) + 0.5
-            update = 0.5 * jnp.tanh(0.5 * (gi_z + gh_z)) + 0.5
-            candidate = jnp.tanh(gi_c + reset * gh_c)
-            previous = mem[rows, cols].astype(F32)
-            renewed = (1.0 - update) * candidate + update * previous
-            out_ref[rows, cols] = jnp.where(count > 0.5, renewed, previous).astype(BF)
-
-    wait_sent(k, messages)
+            moved = dot(place, fresh[:, cols])
+            out_ref[:, cols] = jnp.where(mine, moved, out_ref[:, cols].astype(F32)).astype(BF)
+
+    for c in range(steps):
+        for copy in weight_copies(c):
+            copy.wait()
+        one_step(c)
+    spread(0)
+
+    @pl.loop(1, tiles)
+    def _(t):
+        for c in tile_copies(t):
+            c.start()
+        for c in tile_copies(t):
+            c.wait()
+        for c in range(steps):
+            one_step(c)
+        spread(t * TILE)
 
 
 def on_device(
@@ -328,43 +466,54 @@
     R = max(4, -(-(cap - m) // 4) * 4)
     tr = QUARTERS * R
     QW = DM // QUARTERS
-    mains = max(m, 1) * D if m else 16
+    mains = D * m if m else 16
+    ranks = -(-min(N, D * cap) // TILE) * TILE
     vmem = pl.BlockSpec(memory_space=pltpu.VMEM)
+    smem = pl.BlockSpec(memory_space=pltpu.SMEM)
     anywhere = pl.BlockSpec(memory_space=pl.ANY)
-    return pl.pallas_call(
+    phases = 3 + 2 * HALVES
+    agg, gh, held, rank, total = pl.pallas_call(
         functools.partial(kernel, (D, tm, m, R)),
-        out_shape=jax.ShapeDtypeStruct((N, DM), BF),
-        in_specs=[vmem] * 7 + [anywhere] * 5,
-        out_specs=vmem,
+        out_shape=[
+            jax.ShapeDtypeStruct((ranks, DM), BF),
+            jax.ShapeDtypeStruct((ranks, 3 * DM), F32),
+            jax.ShapeDtypeStruct((ranks, DM), BF),
+            jax.ShapeDtypeStruct((N, 128), I32),
+            jax.ShapeDtypeStruct((8, 128), I32),
+        ],
+        in_specs=[vmem] * 6 + [anywhere] * 4,
+        out_specs=[vmem, anywhere, anywhere, vmem, vmem],
         scratch_shapes=[
             pltpu.VMEM(memory.shape, BF),
             pltpu.VMEM(msg_w1.shape, BF),
             pltpu.VMEM(msg_w2.shape, BF),
-            pltpu.VMEM(gru_in.shape, BF),
             pltpu.VMEM(gru_hid.shape, BF),
-            pltpu.VMEM((N, 3 * DM), F32),
+            pltpu.VMEM((ranks, 3 * DM), F32),
+            pltpu.VMEM((ranks, DM), BF),
             pltpu.VMEM((D * FIELDS, 128), F32),
             pltpu.VMEM((D * FIELDS, 128), F32),
-            pltpu.VMEM((2 * E, DM), BF),
+            pltpu.VMEM((2 * E, DM // HALVES), BF),
+            pltpu.VMEM((E, HID), F32),
             pltpu.VMEM((E, HID), BF),
             pltpu.VMEM((N, 1), F32),
-            pltpu.VMEM((TILE, DM), BF),
             pltpu.VMEM((1, mains), I32),
             pltpu.VMEM((1, mains), F32),
             pltpu.VMEM((1, D * tr), I32),
             pltpu.VMEM((1, D * tr), F32),
             pltpu.VMEM((D * tr, QW), F32),
+            pltpu.VMEM((ranks, DM), F32),
         ]
-        + [pltpu.VMEM((mains, DM), BF)] * 4
+        + [pltpu.VMEM((HALVES, mains, DM // HALVES), BF)] * 4
         + [pltpu.VMEM((D * tr, QW), BF)] * 4
         + [
-            pltpu.SemaphoreType.DMA((5,)),
-            pltpu.SemaphoreType.DMA((5,)),
-            pltpu.SemaphoreType.DMA((5,)),
-            pltpu.SemaphoreType.DMA((5,)),
+            pltpu.SemaphoreType.DMA((4,)),
+            pltpu.SemaphoreType.DMA((phases,)),
+            pltpu.SemaphoreType.DMA((phases,)),
+            pltpu.SemaphoreType.DMA((phases,)),
+            pltpu.SemaphoreType.DMA((2,)),
         ],
         compiler_params=pltpu.CompilerParams(
-            collective_id=0, has_side_effects=True, vmem_limit_bytes=60 * 2**20
+            collective_id=0, has_side_effects=True, vmem_limit_bytes=48 * 2**20
         ),
     )(
         ends_owner.T,
@@ -373,13 +522,27 @@
         edge_feat,
         msg_b1.reshape(1, -1),
         msg_b2.reshape(1, -1),
-        gru_bias.reshape(1, -1),
         memory,
         msg_w1,
         msg_w2,
-        gru_in,
         gru_hid,
     )
+    return pl.pallas_call(
+        gru_kernel,
+        out_shape=jax.ShapeDtypeStruct((N, DM), BF),
+        in_specs=[smem, vmem, vmem, vmem] + [anywhere] * 4,
+        out_specs=vmem,
+        scratch_shapes=[
+            pltpu.VMEM((TILE, DM), BF),
+            pltpu.VMEM((TILE, 3 * DM), F32),
+            pltpu.VMEM((TILE, DM), BF),
+            pltpu.VMEM(gru_in.shape, BF),
+            pltpu.VMEM((TILE, DM), BF),
+            pltpu.SemaphoreType.DMA((3,)),
+            pltpu.SemaphoreType.DMA((DM // TILE, 3)),
+        ],
+        compiler_params=pltpu.CompilerParams(vmem_limit_bytes=40 * 2**20),
+    )(total, rank, gru_bias.reshape(1, -1), memory, agg, gh, held, gru_in)
 
 
 def solution(mesh):

time: 103 us -> 94.2 us (0.915)
  the two profiles are of different devices: /device:TPU:25 before, /device:TPU:0 now
where the time goes in v2:
time: 94.2 us; the launch traced here: 93.8 us
  Pallas kernels  87.7 us (93%)
  local copies, waits for them, and re-layouts  5.85 us (6%)
    pallas_call x1, Pallas kernels, on_device(): pl.pallas_call(functools.partial(kernel, (D, tm, m, R)), out_shape=[jax.S...  79.5 us
    pallas_call x1, Pallas kernels, on_device(): pl.pallas_call(gru_kernel, out_shape=jax.ShapeDtypeStruct((N, DM), BF), i...  8.27 us
    unnamed x20, local copies, waits for them, and re-layouts  5.85 us

profile of v2, /device:TPU:0, one launch (start us, length us, event | category | flops | bytes accessed | tf_op | source)
XLA Modules:
  0.0 93.8 jit_solution(17402279873477495213)
XLA Ops:
  0.0 0.0 copy-start
  0.0 1.6 %copy-done = bf16[1024,1024]{1,0:T(8,128)(2,1)S(1)} copy-done((bf16[1024,1024]{1,0:T(8,128)(2,1)S(1)}, bf16[1024,1024]{1,0:T(8,128)(2,1)}, u32[]{:S(2)}) %copy-start) | copy-done | bytes 2097176
  1.6 0.0 copy-start.3
  1.6 0.8 copy-done.3
  2.4 0.0 copy-start.5
  2.4 0.7 copy-done.5
  3.1 0.0 copy-start.6
  3.1 0.7 copy-done.6
  3.8 0.0 copy-start.7
  3.8 0.7 copy-done.7
  4.5 0.0 copy-start.8
  4.5 0.7 copy-done.8
  5.2 0.0 copy-start.9
  5.2 0.7 copy-done.9
  5.9 0.0 copy-start.1
  5.9 0.0 copy-start.2
  5.9 0.0 copy-start.4
  5.9 79.5 %shard_map.118 = (bf16[768,1024]{1,0:T(8,128)(2,1)S(1)}, f32[768,3072]{1,0:T(8,128)}, bf16[768,1024]{1,0:T(8,128)(2,1)S(1)}, s32[1024,128]{1,0:T(8,128)S(1)}, s32[8,128]{1,0:T(8,128)S(1)}) custom-call(s32[2,256]{1,0:T(2,128)S(1)} %bitcast.9, s32[2,256]{1,0:T(2,128)S(1)} %bitcast.10, s32[1,256]{1,0:T(1,128)S(1)} %bitcast.11, bf16[256,128]{1,0:T(8,128)(2,1)S(1)} %copy-done.3, ...), custom_call_target="tpu_custom_call" | custom-call | tf_op jit(solution)/shard_map/pallas_call | solution.py:475
  85.3 0.0 copy-done.1
  85.4 0.0 copy-done.2
  85.4 0.0 copy-done.4
  85.4 8.3 %shard_map.119 = bf16[1024,1024]{1,0:T(8,128)(2,1)} custom-call(s32[8,128]{1,0:T(8,128)S(1)} %get-tuple-element.10.total_ref, s32[1024,128]{1,0:T(8,128)S(1)} %get-tuple-element.11.rank_ref, f32[1,3072]{1,0:T(1,128)S(1)} %bitcast.6, bf16[1024,1024]{1,0:T(8,128)(2,1)S(1)} %copy-done.1, bf16[768,1024]{1,0:T(8,128)(2,1)S(1)} %get-tuple-element.12.agg_hbm, ...), custom_call_target="tpu_custom_call" | custom-call | tf_op jit(solution)/shard_map/pallas_call | solution.py:530
Async XLA Ops:
  0.0 1.6 %copy-start = (bf16[1024,1024]{1,0:T(8,128)(2,1)S(1)}, bf16[1024,1024]{1,0:T(8,128)(2,1)}, u32[]{:S(2)}) copy-start(bf16[1024,1024]{1,0:T(8,128)(2,1)} %mem_ref.1) | copy-start | bytes 6291460
  1.6 0.8 copy-start.3
  2.4 0.7 copy-start.5
  3.1 0.7 copy-start.6
  3.8 0.7 copy-start.7
  4.5 0.7 copy-start.8
  5.2 0.7 copy-start.9
  5.9 79.5 %copy-start.1 = (bf16[1024,1024]{1,0:T(8,128)(2,1)S(1)}, bf16[1024,1024]{1,0:T(8,128)(2,1)}, u32[]{:S(2)}) copy-start(bf16[1024,1024]{1,0:T(8,128)(2,1)} %mem_ref.1) | copy-start | bytes 6291460
  5.9 79.5 %copy-start.2 = (bf16[1024,3072]{1,0:T(8,128)(2,1)S(1)}, bf16[1024,3072]{1,0:T(8,128)(2,1)}, u32[]{:S(2)}) copy-start(bf16[1024,3072]{1,0:T(8,128)(2,1)} %wi_hbm.1) | copy-start | bytes 18874372
  5.9 79.5 %copy-start.4 = (f32[3072]{0:T(1024)S(1)}, f32[3072]{0:T(1024)}, u32[]{:S(2)}) copy-start(f32[3072]{0:T(1024)} %param.23) | copy-start | bytes 36868

commit v3 on v2

--- a/solution.py
+++ b/solution.py
@@ -52,10 +52,12 @@
 
 def kernel(
     cfg,
-    owner_ref, row_ref, mask_ref, feat_ref, b1_ref, b2_ref,
+    owner_hbm, row_hbm, mask_hbm, feat_hbm, b1_hbm, b2_hbm,
     mem_hbm, w1_hbm, w2_hbm, wh_hbm,
     agg_out, gh_out, held_out, rank_out, total_out,
-    mem, w1, w2, wh, gh, held, table_out, table_in, fetched, acc, hidden, tally,
+    agg, held, rank, total_rows,
+    owner_ref, row_ref, mask_ref, feat_ref, b1_ref, b2_ref,
+    mem, w1, w2, wh, gh, table_out, table_in, fetched, acc, hidden, tally,
     main_row, main_flag, tail_row, tail_flag, tail_acc, sums,
     ans_main, ret_main, msg_main, inc_main, ans_tail, ret_tail, msg_tail, inc_tail,
     load_sem, send_sem, recv_sem, own_sem, store_sem,
@@ -72,7 +74,11 @@
 
     loads = []
     for i, (src, dst) in enumerate(
-        ((mem_hbm, mem), (wh_hbm, wh), (w1_hbm, w1), (w2_hbm, w2))
+        (
+            (owner_hbm, owner_ref), (row_hbm, row_ref), (mask_hbm, mask_ref),
+            (mem_hbm, mem), (wh_hbm, wh), (w1_hbm, w1), (w2_hbm, w2),
+            (feat_hbm, feat_ref), (b1_hbm, b1_ref), (b2_hbm, b2_ref),
+        )
     ):
         c = pltpu.make_async_copy(src, dst, load_sem.at[i])
         c.start()
@@ -126,6 +132,9 @@
     msg_t = [(msg_tail, inc_tail, tr)]
     ans_m = [[(ans_main.at[h], ret_main.at[h], m)] if m else [] for h in range(HALVES)]
     msg_m = [[(msg_main.at[h], inc_main.at[h], m)] if m else [] for h in range(HALVES)]
+
+    for c in loads[:3]:
+        c.wait()
 
     owner = jnp.concatenate([owner_ref[0:1, :], owner_ref[1:2, :]], axis=1)
     wanted = jnp.concatenate([row_ref[0:1, :], row_ref[1:2, :]], axis=1)
@@ -154,7 +163,7 @@
     sent_main = jnp.where(flag[:, E:] > 0, at_main[:, E:], far)
     sent_tail = jnp.where(flag[:, E:] > 0, at_tail[:, E:], far)
 
-    loads[0].wait()
+    loads[3].wait()
     wait_received(0, tables)
 
     table = table_in[...].astype(BF)
@@ -227,8 +236,8 @@
     before = dot(jnp.broadcast_to(touched_row, (8, N)).astype(BF), earlier)[0:1, :]
     rank_row = jnp.where(touched_row > 0.5, before, -1.0)
     rank_column = to_column(rank_row)
-    rank_out[...] = jnp.broadcast_to(rank_column, (N, 128)).astype(I32)
-    total_out[...] = jnp.broadcast_to(
+    rank[...] = jnp.broadcast_to(rank_column, (N, 128)).astype(I32)
+    total_rows[...] = jnp.broadcast_to(
         jnp.sum(touched_row, axis=1, keepdims=True), (8, 128)
     ).astype(I32)
 
@@ -245,7 +254,7 @@
     if m:
         rank_slots(main_row, D * m, main_chunk)
 
-    loads[1].wait()
+    loads[4].wait()
 
     @pl.loop(0, ranks // TILE)
     def _(t):
@@ -265,15 +274,16 @@
         cols = pl.ds(pl.multiple_of(t * TILE, TILE), TILE)
         gh[:, cols] = dot(held[...], wh[:, cols])
 
-    stores = [
-        pltpu.make_async_copy(gh, gh_out, store_sem.at[0]),
-        pltpu.make_async_copy(held, held_out, store_sem.at[1]),
-    ]
-    for c in stores:
+    stores = []
+    for i, (src, dst) in enumerate(
+        ((gh, gh_out), (held, held_out), (rank, rank_out), (total_rows, total_out))
+    ):
+        c = pltpu.make_async_copy(src, dst, store_sem.at[i])
         c.start()
-
-    loads[2].wait()
-    loads[3].wait()
+        stores.append(c)
+
+    for c in loads[5:]:
+        c.wait()
     feat_width = feat_ref.shape[1]
 
     @pl.loop(0, HID // TILE)
@@ -357,89 +367,123 @@
             summed = dot(hit, inc_tail[...])
             if m:
                 summed = summed + sums[rows, cols]
-            agg_out[rows, cols] = (summed / count).astype(BF)
-
+            agg[rows, cols] = (summed / count).astype(BF)
+        pltpu.make_async_copy(agg.at[rows], agg_out.at[rows], store_sem.at[len(stores)]).start()
+
+    pltpu.make_async_copy(agg, agg_out, store_sem.at[len(stores)]).wait()
     wait_sent(k, msg_t)
     for h in range(HALVES):
         wait_sent(k + 1 + h, msg_m[h])
 
 
 def gru_kernel(
-    total_ref, rank_ref, gb_ref, mem_ref, agg_hbm, gh_hbm, held_hbm, wi_hbm,
-    out_ref,
-    agg, gh, held, wi, fresh, load_sem, weight_sem,
+    total_ref, rank_hbm, gb_hbm, mem_hbm, agg_hbm, held_hbm, wi_hbm, gh_hbm,
+    out_hbm,
+    rank_ref, gb_ref, mem, agg, held, wi, gh, fresh, out,
+    small_sem, tile_sem, weight_sem, gate_sem, mem_sem, out_sem,
 ):
-    N, DM = mem_ref.shape
+    N, DM = mem.shape
     steps = DM // TILE
     tiles = lax.div(total_ref[0, 0] + (TILE - 1), TILE)
 
-    def tile_copies(t):
-        rows = pl.ds(pl.multiple_of(t * TILE, TILE), TILE)
+    def columns(c, gate=0):
+        return slice(gate * DM + c * TILE, gate * DM + (c + 1) * TILE)
+
+    def tile_copies(base):
+        rows = pl.ds(base, TILE)
         return [
-            pltpu.make_async_copy(agg_hbm.at[rows], agg, load_sem.at[0]),
-            pltpu.make_async_copy(gh_hbm.at[rows], gh, load_sem.at[1]),
-            pltpu.make_async_copy(held_hbm.at[rows], held, load_sem.at[2]),
+            pltpu.make_async_copy(agg_hbm.at[rows], agg, tile_sem.at[0]),
+            pltpu.make_async_copy(held_hbm.at[rows], held, tile_sem.at[1]),
         ]
 
+    def gate_copies(base, c):
+        return [
+            pltpu.make_async_copy(
+                gh_hbm.at[pl.ds(base, TILE), columns(c, g)], gh.at[:, columns(c, g)],
+                gate_sem.at[c, g],
+            )
+            for g in range(3)
+        ]
+
     def weight_copies(c):
-        copies = []
-        for g in range(3):
-            cols = pl.ds(g * DM + c * TILE, TILE)
-            copies.append(
-                pltpu.make_async_copy(wi_hbm.at[:, cols], wi.at[:, cols], weight_sem.at[c, g])
+        return [
+            pltpu.make_async_copy(
+                wi_hbm.at[:, columns(c, g)], wi.at[:, columns(c, g)], weight_sem.at[c, g]
             )
-        return copies
-
-    for c in tile_copies(0):
-        c.start()
-    for c in range(steps):
-        for copy in weight_copies(c):
-            copy.start()
-    out_ref[...] = mem_ref[...]
-    for c in tile_copies(0):
-        c.wait()
-
-    def one_step(c):
-        def part(g):
-            cols = slice(g * DM + c * TILE, g * DM + (c + 1) * TILE)
-            return dot(agg[...], wi[:, cols]) + gb_ref[:, cols], gh[:, cols]
-
-        cols = slice(c * TILE, (c + 1) * TILE)
-        gi_r, gh_r = part(0)
-        gi_z, gh_z = part(1)
-        gi_c, gh_c = part(2)
-        reset = 0.5 * jnp.tanh(0.5 * (gi_r + gh_r)) + 0.5
-        update = 0.5 * jnp.tanh(0.5 * (gi_z + gh_z)) + 0.5
-        candidate = jnp.tanh(gi_c + reset * gh_c)
-        previous = held[:, cols].astype(F32)
-        fresh[:, cols] = ((1.0 - update) * candidate + update * previous).astype(BF)
-
-    def spread(base):
+            for g in range(3)
+        ]
+
+    def mem_copy(c):
+        return pltpu.make_async_copy(
+            mem_hbm.at[:, columns(c)], mem.at[:, columns(c)], mem_sem.at[c]
+        )
+
+    def out_copy(c):
+        return pltpu.make_async_copy(
+            out.at[:, columns(c)], out_hbm.at[:, columns(c)], out_sem.at[c]
+        )
+
+    small = [
+        pltpu.make_async_copy(gb_hbm, gb_ref, small_sem.at[0]),
+        pltpu.make_async_copy(rank_hbm, rank_ref, small_sem.at[1]),
+    ]
+
+    def tile(t):
+        first = isinstance(t, int)
+        base = t * TILE if first else pl.multiple_of(t * TILE, TILE)
+        for c in tile_copies(base):
+            c.start()
+        for c in range(steps):
+            if first:
+                for copy in weight_copies(c):
+                    copy.start()
+                if c == 0:
+                    for copy in small:
+                        copy.start()
+            for copy in gate_copies(base, c):
+                copy.start()
+            if first:
+                mem_copy(c).start()
+        for c in tile_copies(base):
+            c.wait()
+        if first:
+            for copy in small:
+                copy.wait()
         column = rank_ref[:, 0:1] - base
         place = ones_where(column == iota(N, TILE, 1))
         mine = (column >= 0) & (column < TILE)
-
-        @pl.loop(0, steps)
-        def _(c):
-            cols = pl.ds(pl.multiple_of(c * TILE, TILE), TILE)
-            moved = dot(place, fresh[:, cols])
-            out_ref[:, cols] = jnp.where(mine, moved, out_ref[:, cols].astype(F32)).astype(BF)
-
-    for c in range(steps):
-        for copy in weight_copies(c):
-            copy.wait()
-        one_step(c)
-    spread(0)
+        for c in range(steps):
+            if first:
+                for copy in weight_copies(c):
+                    copy.wait()
+            gates = [
+                dot(agg[...], wi[:, columns(c, g)]) + gb_ref[:, columns(c, g)] for g in range(3)
+            ]
+            for copy in gate_copies(base, c):
+                copy.wait()
+            reset = 0.5 * jnp.tanh(0.5 * (gates[0] + gh[:, columns(c, 0)])) + 0.5
+            update = 0.5 * jnp.tanh(0.5 * (gates[1] + gh[:, columns(c, 1)])) + 0.5
+            candidate = jnp.tanh(gates[2] + reset * gh[:, columns(c, 2)])
+            previous = held[:, columns(c)].astype(F32)
+            fresh[:, columns(c)] = ((1.0 - update) * candidate + update * previous).astype(BF)
+            moved = dot(place, fresh[:, columns(c)])
+            if first:
+                mem_copy(c).wait()
+            before = mem[:, columns(c)] if first else out[:, columns(c)]
+            out[:, columns(c)] = jnp.where(mine, moved, before.astype(F32)).astype(BF)
+
+            @pl.when(tiles <= 1 if first else t == tiles - 1)
+            def _():
+                out_copy(c).start()
+
+    tile(0)
 
     @pl.loop(1, tiles)
     def _(t):
-        for c in tile_copies(t):
-            c.start()
-        for c in tile_copies(t):
-            c.wait()
-        for c in range(steps):
-            one_step(c)
-        spread(t * TILE)
+        tile(t)
+
+    for c in range(steps):
+        out_copy(c).wait()
 
 
 def on_device(
@@ -468,9 +512,8 @@
     QW = DM // QUARTERS
     mains = D * m if m else 16
     ranks = -(-min(N, D * cap) // TILE) * TILE
-    vmem = pl.BlockSpec(memory_space=pltpu.VMEM)
     smem = pl.BlockSpec(memory_space=pltpu.SMEM)
-    anywhere = pl.BlockSpec(memory_space=pl.ANY)
+    hbm = pl.BlockSpec(memory_space=pltpu.HBM)
     phases = 3 + 2 * HALVES
     agg, gh, held, rank, total = pl.pallas_call(
         functools.partial(kernel, (D, tm, m, R)),
@@ -481,15 +524,24 @@
             jax.ShapeDtypeStruct((N, 128), I32),
             jax.ShapeDtypeStruct((8, 128), I32),
         ],
-        in_specs=[vmem] * 6 + [anywhere] * 4,
-        out_specs=[vmem, anywhere, anywhere, vmem, vmem],
+        in_specs=[hbm] * 10,
+        out_specs=[hbm] * 5,
         scratch_shapes=[
+            pltpu.VMEM((ranks, DM), BF),
+            pltpu.VMEM((ranks, DM), BF),
+            pltpu.VMEM((N, 128), I32),
+            pltpu.VMEM((8, 128), I32),
+            pltpu.VMEM((2, E), I32),
+            pltpu.VMEM((2, E), I32),
+            pltpu.VMEM((1, E), I32),
+            pltpu.VMEM(edge_feat.shape, BF),
+            pltpu.VMEM((1, HID), F32),
+            pltpu.VMEM((1, DM), F32),
             pltpu.VMEM(memory.shape, BF),
             pltpu.VMEM(msg_w1.shape, BF),
             pltpu.VMEM(msg_w2.shape, BF),
             pltpu.VMEM(gru_hid.shape, BF),
             pltpu.VMEM((ranks, 3 * DM), F32),
-            pltpu.VMEM((ranks, DM), BF),
             pltpu.VMEM((D * FIELDS, 128), F32),
             pltpu.VMEM((D * FIELDS, 128), F32),
             pltpu.VMEM((2 * E, DM // HALVES), BF),
@@ -506,14 +558,14 @@
         + [pltpu.VMEM((HALVES, mains, DM // HALVES), BF)] * 4
         + [pltpu.VMEM((D * tr, QW), BF)] * 4
         + [
-            pltpu.SemaphoreType.DMA((4,)),
+            pltpu.SemaphoreType.DMA((10,)),
             pltpu.SemaphoreType.DMA((phases,)),
             pltpu.SemaphoreType.DMA((phases,)),
             pltpu.SemaphoreType.DMA((phases,)),
-            pltpu.SemaphoreType.DMA((2,)),
+            pltpu.SemaphoreType.DMA((5,)),
         ],
         compiler_params=pltpu.CompilerParams(
-            collective_id=0, has_side_effects=True, vmem_limit_bytes=48 * 2**20
+            collective_id=0, has_side_effects=True, vmem_limit_bytes=60 * 2**20
         ),
     )(
         ends_owner.T,
@@ -530,19 +582,27 @@
     return pl.pallas_call(
         gru_kernel,
         out_shape=jax.ShapeDtypeStruct((N, DM), BF),
-        in_specs=[smem, vmem, vmem, vmem] + [anywhere] * 4,
-        out_specs=vmem,
+        in_specs=[smem] + [hbm] * 7,
+        out_specs=hbm,
         scratch_shapes=[
+            pltpu.VMEM((N, 128), I32),
+            pltpu.VMEM((1, 3 * DM), F32),
+            pltpu.VMEM((N, DM), BF),
             pltpu.VMEM((TILE, DM), BF),
+            pltpu.VMEM((TILE, DM), BF),
+            pltpu.VMEM(gru_in.shape, BF),
             pltpu.VMEM((TILE, 3 * DM), F32),
             pltpu.VMEM((TILE, DM), BF),
-            pltpu.VMEM(gru_in.shape, BF),
-            pltpu.VMEM((TILE, DM), BF),
-            pltpu.SemaphoreType.DMA((3,)),
+            pltpu.VMEM((N, DM), BF),
+            pltpu.SemaphoreType.DMA((2,)),
+            pltpu.SemaphoreType.DMA((2,)),
             pltpu.SemaphoreType.DMA((DM // TILE, 3)),
+            pltpu.SemaphoreType.DMA((DM // TILE, 3)),
+            pltpu.SemaphoreType.DMA((DM // TILE,)),
+            pltpu.SemaphoreType.DMA((DM // TILE,)),
         ],
-        compiler_params=pltpu.CompilerParams(vmem_limit_bytes=40 * 2**20),
-    )(total, rank, gru_bias.reshape(1, -1), memory, agg, gh, held, gru_in)
+        compiler_params=pltpu.CompilerParams(vmem_limit_bytes=60 * 2**20),
+    )(total, rank, gru_bias.reshape(1, -1), memory, agg, held, gru_in, gh)
 
 
 def solution(mesh):

time: 94.2 us -> 92.9 us (0.986)
  local copies, waits for them, and re-layouts: 5.85 us -> 0 us
  Pallas kernels: 87.7 us -> 92.5 us
    unnamed x20 -> x0, local copies, waits for them, and re-layouts: 5.85 us -> none
    pallas_call x1, Pallas kernels: 8.27 us -> 12.3 us  [on_device(): pl.pallas_call(gru_kernel, out_shape=jax.ShapeDtypeStruct((N, DM), BF), i...]
where the time goes in v3:
time: 92.9 us; the launch traced here: 92.7 us
  Pallas kernels  92.5 us (100%)
    pallas_call x1, Pallas kernels, on_device(): pl.pallas_call(functools.partial(kernel, (D, tm, m, R)), out_shape=[jax.S...  80.2 us
    pallas_call x1, Pallas kernels, on_device(): pl.pallas_call(gru_kernel, out_shape=jax.ShapeDtypeStruct((N, DM), BF), i...  12.3 us

profile of v3, /device:TPU:0, one launch (start us, length us, event | category | flops | bytes accessed | tf_op | source)
XLA Modules:
  0.0 92.7 jit_solution(8096436892667508555)
XLA Ops:
  0.0 80.2 %shard_map.118 = (bf16[768,1024]{1,0:T(8,128)(2,1)}, f32[768,3072]{1,0:T(8,128)}, bf16[768,1024]{1,0:T(8,128)(2,1)}, s32[1024,128]{1,0:T(8,128)}, s32[8,128]{1,0:T(8,128)}) custom-call(s32[2,256]{1,0:T(2,128)} %bitcast.9, s32[2,256]{1,0:T(2,128)} %bitcast.10, s32[1,256]{1,0:T(1,128)} %bitcast.11, bf16[256,128]{1,0:T(8,128)(2,1)} %feat_hbm.1, ...), custom_call_target="tpu_custom_call" | custom-call | tf_op jit(solution)/shard_map/pallas_call | solution.py:518
  80.3 12.3 %shard_map.119 = bf16[1024,1024]{1,0:T(8,128)(2,1)} custom-call(s32[8,128]{1,0:T(8,128)} %get-tuple-element.10.total_ref, s32[1024,128]{1,0:T(8,128)} %get-tuple-element.11.rank_hbm, f32[1,3072]{1,0:T(1,128)} %bitcast.6, bf16[1024,1024]{1,0:T(8,128)(2,1)} %mem_hbm.3, bf16[768,1024]{1,0:T(8,128)(2,1)} %get-tuple-element.12.agg_hbm, ...), custom_call_target="tpu_custom_call" | custom-call | tf_op jit(solution)/shard_map/pallas_call | solution.py:582

commit v4 on v3

--- a/solution.py
+++ b/solution.py
@@ -53,12 +53,12 @@
 def kernel(
     cfg,
     owner_hbm, row_hbm, mask_hbm, feat_hbm, b1_hbm, b2_hbm,
-    mem_hbm, w1_hbm, w2_hbm, wh_hbm,
-    agg_out, gh_out, held_out, rank_out, total_out,
-    agg, held, rank, total_rows,
+    mem_hbm, w1_hbm, w2_hbm, wh_hbm, wi_hbm, gb_hbm,
+    agg_out, gh_out, held_out, rank_out, total_out, fresh_out,
+    agg, held, rank, total_rows, fresh, wi, gb_ref, from_tail, sum_main, sum_tail,
     owner_ref, row_ref, mask_ref, feat_ref, b1_ref, b2_ref,
     mem, w1, w2, wh, gh, table_out, table_in, fetched, acc, hidden, tally,
-    main_row, main_flag, tail_row, tail_flag, tail_acc, sums,
+    main_row, main_flag, tail_row, tail_flag, sums,
     ans_main, ret_main, msg_main, inc_main, ans_tail, ret_tail, msg_tail, inc_tail,
     load_sem, send_sem, recv_sem, own_sem, store_sem,
 ):
@@ -78,6 +78,7 @@
             (owner_hbm, owner_ref), (row_hbm, row_ref), (mask_hbm, mask_ref),
             (mem_hbm, mem), (wh_hbm, wh), (w1_hbm, w1), (w2_hbm, w2),
             (feat_hbm, feat_ref), (b1_hbm, b1_ref), (b2_hbm, b2_ref),
+            (wi_hbm, wi), (gb_hbm, gb_ref),
         )
     ):
         c = pltpu.make_async_copy(src, dst, load_sem.at[i])
@@ -182,6 +183,25 @@
         return ids - 32.0, marks
 
     chunk = min(512, D * tr)
+    main_chunk = min(512, D * m)
+
+    def answer_main(h):
+        @pl.loop(0, D * m // main_chunk)
+        def _(step):
+            base = pl.multiple_of(step * main_chunk, main_chunk)
+            ids, marks = slots(base, main_chunk, m, 0, m)
+            if h == 1:
+                main_row[:, pl.ds(base, main_chunk)] = to_row(ids).astype(I32)
+                main_flag[:, pl.ds(base, main_chunk)] = to_row(marks)
+            hit = ones_where(iota(main_chunk, N, 1) == ids.astype(I32))
+            ans_main[h, pl.ds(base, main_chunk), :] = dot(
+                hit, mem[:, h * HW : (h + 1) * HW]
+            ).astype(BF)
+
+        start_exchange(2 + h, ans_m[h])
+
+    if m:
+        answer_main(0)
 
     @pl.loop(0, D * tr // chunk)
     def _(step):
@@ -191,32 +211,14 @@
         tail_row[:, pl.ds(base, chunk)] = to_row(ids).astype(I32)
         tail_flag[:, pl.ds(base, chunk)] = to_row(jnp.where(quarter == 0, marks, 0.0))
         total = jnp.zeros((chunk, QW), F32)
-        nodes = iota(chunk, N, 1)
+        hit = ones_where(iota(chunk, N, 1) == ids.astype(I32))
         for q in range(QUARTERS):
-            hit = ones_where(nodes == jnp.where(quarter == q, ids.astype(I32), -1))
-            total = total + dot(hit, mem[:, q * QW : (q + 1) * QW])
+            total = total + jnp.where(quarter == q, dot(hit, mem[:, q * QW : (q + 1) * QW]), 0.0)
         ans_tail[pl.ds(base, chunk), :] = total.astype(BF)
 
     start_exchange(1, ans_t)
-
     if m:
-        main_chunk = min(512, D * m)
-        main_steps = D * m // main_chunk
-        for h in range(HALVES):
-
-            @pl.loop(0, main_steps)
-            def _(step):
-                base = pl.multiple_of(step * main_chunk, main_chunk)
-                ids, marks = slots(base, main_chunk, m, 0, m)
-                if h == 0:
-                    main_row[:, pl.ds(base, main_chunk)] = to_row(ids).astype(I32)
-                    main_flag[:, pl.ds(base, main_chunk)] = to_row(marks)
-                hit = ones_where(iota(main_chunk, N, 1) == ids.astype(I32))
-                ans_main[h, pl.ds(base, main_chunk), :] = dot(
-                    hit, mem[:, h * HW : (h + 1) * HW]
-                ).astype(BF)
-
-            start_exchange(2 + h, ans_m[h])
+        answer_main(1)
 
     @pl.loop(0, N // TILE)
     def _(t):
@@ -282,7 +284,7 @@
         c.start()
         stores.append(c)
 
-    for c in loads[5:]:
+    for c in loads[5:10]:
         c.wait()
     feat_width = feat_ref.shape[1]
 
@@ -291,15 +293,31 @@
         cols = pl.ds(pl.multiple_of(t * TILE, TILE), TILE)
         acc[:, cols] = dot(feat_ref[...], w1[2 * DM : 2 * DM + feat_width, cols]) + b1_ref[:, cols]
 
-    wait_received(1, ans_t)
+    quarter_row = rem(div(iota(1, D * tr, 1), R), QUARTERS)
+    quarter_column = rem(div(iota(D * tr, 1, 0), R), QUARTERS)
+    lane = iota(1, D * tr, 1) - quarter_row * R
+    from_tail[...] = ones_where(jnp.broadcast_to(lane, (2 * E, D * tr)) == tail_column)
     if m:
         from_main = ones_where(iota(2 * E, D * m, 1) == main_column)
 
+    @pl.loop(0, ranks // TILE)
+    def _(t):
+        base = pl.multiple_of(t * TILE, TILE)
+        rows = pl.ds(base, TILE)
+        sum_tail[rows, :] = ones_where(tail_row[...] == base + iota(TILE, D * tr, 0))
+        if m:
+            sum_main[rows, :] = ones_where(main_row[...] == base + iota(TILE, D * m, 0))
+
+    def of_quarter(ref, q):
+        return ref[...] * ones_where(quarter_column == q)
+
     for h in range(HALVES):
         wait_received(2 + h, ans_m[h])
+        if h == 0:
+            wait_received(1, ans_t)
         got = []
         for q in range(h * QUARTERS // HALVES, (h + 1) * QUARTERS // HALVES):
-            got.append(dot(ones_where(iota(2 * E, D * tr, 1) == tail_column + q * R), ret_tail[...]))
+            got.append(dot(from_tail[...], of_quarter(ret_tail, q)))
         got = jnp.concatenate(got, axis=1)
         if m:
             got = got + dot(from_main, ret_main[h])
@@ -315,7 +333,7 @@
             else:
                 acc[:, cols] = total
 
-    tail_acc[...] = jnp.zeros_like(tail_acc)
+    to_tail = ones_where(iota(D * tr, E, 0) - quarter_column * R == sent_tail)
     if m:
         to_main = ones_where(iota(D * m, E, 0) == sent_main)
     k = 2 + HALVES
@@ -325,14 +343,13 @@
         if m:
             msg_main[h] = dot(to_main, message).astype(BF)
             start_exchange(k + 1 + h, msg_m[h])
+        moved = dot(to_tail, message)
         for j in range(QUARTERS // HALVES):
-            q = h * QUARTERS // HALVES + j
-            tail_acc[...] += dot(
-                ones_where(iota(D * tr, E, 0) == sent_tail + q * R),
-                message[:, j * QW : (j + 1) * QW],
-            )
-
-    msg_tail[...] = tail_acc[...].astype(BF)
+            part = jnp.where(
+                quarter_column == h * QUARTERS // HALVES + j, moved[:, j * QW : (j + 1) * QW], 0.0
+            ).astype(BF)
+            msg_tail[...] = part if h == 0 and j == 0 else msg_tail[...] + part
+
     start_exchange(k, msg_t)
     wait_sent(0, tables)
     wait_sent(1, ans_t)
@@ -341,77 +358,72 @@
     for c in stores:
         c.wait()
 
-    quarter = rem(div(iota(1, D * tr, 1), R), QUARTERS)
+    loads[10].wait()
+    loads[11].wait()
+
     for h in range(HALVES):
         wait_received(k + 1 + h, msg_m[h])
-        if h == HALVES - 1:
-            wait_received(k, msg_t)
         if m:
 
             @pl.loop(0, ranks // TILE)
             def _(t):
-                base = pl.multiple_of(t * TILE, TILE)
-                rows = pl.ds(base, TILE)
-                hit = ones_where(main_row[...] == base + iota(TILE, D * m, 0))
-                sums[rows, h * HW : (h + 1) * HW] = dot(hit, inc_main[h])
-
-    @pl.loop(0, ranks // TILE)
-    def _(t):
-        base = pl.multiple_of(t * TILE, TILE)
-        rows = pl.ds(base, TILE)
-        count = jnp.maximum(tally[rows, :], 1.0)
-        for q in range(QUARTERS):
-            cols = slice(q * QW, (q + 1) * QW)
-            wanted_rank = base + iota(TILE, D * tr, 0)
-            hit = ones_where(jnp.where(quarter == q, tail_row[...], -1) == wanted_rank)
-            summed = dot(hit, inc_tail[...])
+                rows = pl.ds(pl.multiple_of(t * TILE, TILE), TILE)
+                sums[rows, h * HW : (h + 1) * HW] = dot(sum_main[rows, :], inc_main[h])
+
+    wait_received(k, msg_t)
+    for q in range(QUARTERS):
+        cols = slice(q * QW, (q + 1) * QW)
+        part = of_quarter(inc_tail, q)
+        for t in range(ranks // TILE):
+            rows = slice(t * TILE, (t + 1) * TILE)
+            summed = dot(sum_tail[rows, :], part)
             if m:
                 summed = summed + sums[rows, cols]
-            agg[rows, cols] = (summed / count).astype(BF)
-        pltpu.make_async_copy(agg.at[rows], agg_out.at[rows], store_sem.at[len(stores)]).start()
-
-    pltpu.make_async_copy(agg, agg_out, store_sem.at[len(stores)]).wait()
+            agg[rows, cols] = (summed / jnp.maximum(tally[rows, :], 1.0)).astype(BF)
+    last = pltpu.make_async_copy(agg, agg_out, store_sem.at[4])
+    last.start()
+
+    copies = []
+    for c in range(DM // TILE):
+        cols = slice(c * TILE, (c + 1) * TILE)
+        fresh[:, cols] = gru_columns(agg[0:TILE, :], wi, gb_ref, gh, held, c)
+        copy = pltpu.make_async_copy(fresh.at[:, cols], fresh_out.at[:, cols], store_sem.at[5 + c])
+        copy.start()
+        copies.append(copy)
+    last.wait()
+    for copy in copies:
+        copy.wait()
     wait_sent(k, msg_t)
     for h in range(HALVES):
         wait_sent(k + 1 + h, msg_m[h])
 
 
-def gru_kernel(
-    total_ref, rank_hbm, gb_hbm, mem_hbm, agg_hbm, held_hbm, wi_hbm, gh_hbm,
+def gru_columns(agg, wi, gb, gh, held, c):
+    DM = agg.shape[1]
+    gates, hid = [], []
+    for g in range(3):
+        part = slice(g * DM + c * TILE, g * DM + (c + 1) * TILE)
+        gates.append(dot(agg, wi[:, part]) + gb[:, part])
+        hid.append(gh[0:TILE, part])
+    reset = 0.5 * jnp.tanh(0.5 * (gates[0] + hid[0])) + 0.5
+    update = 0.5 * jnp.tanh(0.5 * (gates[1] + hid[1])) + 0.5
+    candidate = jnp.tanh(gates[2] + reset * hid[2])
+    previous = held[0:TILE, c * TILE : (c + 1) * TILE].astype(F32)
+    return ((1.0 - update) * candidate + update * previous).astype(BF)
+
+
+def place_kernel(
+    total_ref, rank_hbm, gb_hbm, mem_hbm, agg_hbm, held_hbm, wi_hbm, gh_hbm, fresh_hbm,
     out_hbm,
     rank_ref, gb_ref, mem, agg, held, wi, gh, fresh, out,
-    small_sem, tile_sem, weight_sem, gate_sem, mem_sem, out_sem,
+    first_sem, tile_sem, mem_sem, out_sem,
 ):
     N, DM = mem.shape
     steps = DM // TILE
     tiles = lax.div(total_ref[0, 0] + (TILE - 1), TILE)
 
-    def columns(c, gate=0):
-        return slice(gate * DM + c * TILE, gate * DM + (c + 1) * TILE)
-
-    def tile_copies(base):
-        rows = pl.ds(base, TILE)
-        return [
-            pltpu.make_async_copy(agg_hbm.at[rows], agg, tile_sem.at[0]),
-            pltpu.make_async_copy(held_hbm.at[rows], held, tile_sem.at[1]),
-        ]
-
-    def gate_copies(base, c):
-        return [
-            pltpu.make_async_copy(
-                gh_hbm.at[pl.ds(base, TILE), columns(c, g)], gh.at[:, columns(c, g)],
-                gate_sem.at[c, g],
-            )
-            for g in range(3)
-        ]
-
-    def weight_copies(c):
-        return [
-            pltpu.make_async_copy(
-                wi_hbm.at[:, columns(c, g)], wi.at[:, columns(c, g)], weight_sem.at[c, g]
-            )
-            for g in range(3)
-        ]
+    def columns(c):
+        return slice(c * TILE, (c + 1) * TILE)
 
     def mem_copy(c):
         return pltpu.make_async_copy(
@@ -423,64 +435,50 @@
             out.at[:, columns(c)], out_hbm.at[:, columns(c)], out_sem.at[c]
         )
 
-    small = [
-        pltpu.make_async_copy(gb_hbm, gb_ref, small_sem.at[0]),
-        pltpu.make_async_copy(rank_hbm, rank_ref, small_sem.at[1]),
+    def place(base, c, before):
+        column = rank_ref[:, 0:1] - base
+        moved = dot(ones_where(column == iota(N, TILE, 1)), fresh[:, columns(c)])
+        mine = (column >= 0) & (column < TILE)
+        out[:, columns(c)] = jnp.where(mine, moved, before[:, columns(c)].astype(F32)).astype(BF)
+
+    starts = [
+        pltpu.make_async_copy(rank_hbm, rank_ref, first_sem.at[0]),
+        pltpu.make_async_copy(fresh_hbm, fresh, first_sem.at[1]),
     ]
-
-    def tile(t):
-        first = isinstance(t, int)
-        base = t * TILE if first else pl.multiple_of(t * TILE, TILE)
-        for c in tile_copies(base):
-            c.start()
+    for c in starts:
+        c.start()
+    for c in range(steps):
+        mem_copy(c).start()
+    for c in starts:
+        c.wait()
+    for c in range(steps):
+        mem_copy(c).wait()
+        place(0, c, mem)
+
+        @pl.when(tiles <= 1)
+        def _():
+            out_copy(c).start()
+
+    @pl.loop(1, tiles)
+    def _(t):
+        base = pl.multiple_of(t * TILE, TILE)
+        rows = pl.ds(base, TILE)
+        pairs = (
+            (agg_hbm.at[rows], agg), (held_hbm.at[rows], held), (gh_hbm.at[rows], gh),
+            (wi_hbm, wi), (gb_hbm, gb_ref),
+        )
+        copies = [pltpu.make_async_copy(a, b, tile_sem.at[i]) for i, (a, b) in enumerate(pairs)]
+        for copy in copies:
+            copy.start()
+        for copy in copies:
+            copy.wait()
         for c in range(steps):
-            if first:
-                for copy in weight_copies(c):
-                    copy.start()
-                if c == 0:
-                    for copy in small:
-                        copy.start()
-            for copy in gate_copies(base, c):
-                copy.start()
-            if first:
-                mem_copy(c).start()
-        for c in tile_copies(base):
-            c.wait()
-        if first:
-            for copy in small:
-                copy.wait()
-        column = rank_ref[:, 0:1] - base
-        place = ones_where(column == iota(N, TILE, 1))
-        mine = (column >= 0) & (column < TILE)
-        for c in range(steps):
-            if first:
-                for copy in weight_copies(c):
-                    copy.wait()
-            gates = [
-                dot(agg[...], wi[:, columns(c, g)]) + gb_ref[:, columns(c, g)] for g in range(3)
-            ]
-            for copy in gate_copies(base, c):
-                copy.wait()
-            reset = 0.5 * jnp.tanh(0.5 * (gates[0] + gh[:, columns(c, 0)])) + 0.5
-            update = 0.5 * jnp.tanh(0.5 * (gates[1] + gh[:, columns(c, 1)])) + 0.5
-            candidate = jnp.tanh(gates[2] + reset * gh[:, columns(c, 2)])
-            previous = held[:, columns(c)].astype(F32)
-            fresh[:, columns(c)] = ((1.0 - update) * candidate + update * previous).astype(BF)
-            moved = dot(place, fresh[:, columns(c)])
-            if first:
-                mem_copy(c).wait()
-            before = mem[:, columns(c)] if first else out[:, columns(c)]
-            out[:, columns(c)] = jnp.where(mine, moved, before.astype(F32)).astype(BF)
-
-            @pl.when(tiles <= 1 if first else t == tiles - 1)
+            fresh[:, columns(c)] = gru_columns(agg[...], wi, gb_ref, gh, held, c)
+            place(base, c, out)
+
+            @pl.when(t == tiles - 1)
             def _():
                 out_copy(c).start()
-
-    tile(0)
-
-    @pl.loop(1, tiles)
-    def _(t):
-        tile(t)
 
     for c in range(steps):
         out_copy(c).wait()
@@ -515,7 +513,7 @@
     smem = pl.BlockSpec(memory_space=pltpu.SMEM)
     hbm = pl.BlockSpec(memory_space=pltpu.HBM)
     phases = 3 + 2 * HALVES
-    agg, gh, held, rank, total = pl.pallas_call(
+    agg, gh, held, rank, total, fresh = pl.pallas_call(
         functools.partial(kernel, (D, tm, m, R)),
         out_shape=[
             jax.ShapeDtypeStruct((ranks, DM), BF),
@@ -523,14 +521,21 @@
             jax.ShapeDtypeStruct((ranks, DM), BF),
             jax.ShapeDtypeStruct((N, 128), I32),
             jax.ShapeDtypeStruct((8, 128), I32),
+            jax.ShapeDtypeStruct((TILE, DM), BF),
         ],
-        in_specs=[hbm] * 10,
-        out_specs=[hbm] * 5,
+        in_specs=[hbm] * 12,
+        out_specs=[hbm] * 6,
         scratch_shapes=[
             pltpu.VMEM((ranks, DM), BF),
             pltpu.VMEM((ranks, DM), BF),
             pltpu.VMEM((N, 128), I32),
             pltpu.VMEM((8, 128), I32),
+            pltpu.VMEM((TILE, DM), BF),
+            pltpu.VMEM(gru_in.shape, BF),
+            pltpu.VMEM((1, 3 * DM), F32),
+            pltpu.VMEM((2 * E, D * tr), BF),
+            pltpu.VMEM((ranks if m else 16, mains), BF),
+            pltpu.VMEM((ranks, D * tr), BF),
             pltpu.VMEM((2, E), I32),
             pltpu.VMEM((2, E), I32),
             pltpu.VMEM((1, E), I32),
@@ -552,17 +557,16 @@
             pltpu.VMEM((1, mains), F32),
             pltpu.VMEM((1, D * tr), I32),
             pltpu.VMEM((1, D * tr), F32),
-            pltpu.VMEM((D * tr, QW), F32),
-            pltpu.VMEM((ranks, DM), F32),
+            pltpu.VMEM((ranks if m else 8, DM), F32),
         ]
         + [pltpu.VMEM((HALVES, mains, DM // HALVES), BF)] * 4
         + [pltpu.VMEM((D * tr, QW), BF)] * 4
         + [
-            pltpu.SemaphoreType.DMA((10,)),
+            pltpu.SemaphoreType.DMA((12,)),
             pltpu.SemaphoreType.DMA((phases,)),
             pltpu.SemaphoreType.DMA((phases,)),
             pltpu.SemaphoreType.DMA((phases,)),
-            pltpu.SemaphoreType.DMA((5,)),
+            pltpu.SemaphoreType.DMA((5 + DM // TILE,)),
         ],
         compiler_params=pltpu.CompilerParams(
             collective_id=0, has_side_effects=True, vmem_limit_bytes=60 * 2**20
@@ -578,11 +582,13 @@
         msg_w1,
         msg_w2,
         gru_hid,
+        gru_in,
+        gru_bias.reshape(1, -1),
     )
     return pl.pallas_call(
-        gru_kernel,
+        place_kernel,
         out_shape=jax.ShapeDtypeStruct((N, DM), BF),
-        in_specs=[smem] + [hbm] * 7,
+        in_specs=[smem] + [hbm] * 8,
         out_specs=hbm,
         scratch_shapes=[
             pltpu.VMEM((N, 128), I32),
@@ -595,14 +601,12 @@
             pltpu.VMEM((TILE, DM), BF),
             pltpu.VMEM((N, DM), BF),
             pltpu.SemaphoreType.DMA((2,)),
-            pltpu.SemaphoreType.DMA((2,)),
-            pltpu.SemaphoreType.DMA((DM // TILE, 3)),
-            pltpu.SemaphoreType.DMA((DM // TILE, 3)),
+            pltpu.SemaphoreType.DMA((5,)),
             pltpu.SemaphoreType.DMA((DM // TILE,)),
             pltpu.SemaphoreType.DMA((DM // TILE,)),
         ],
         compiler_params=pltpu.CompilerParams(vmem_limit_bytes=60 * 2**20),
-    )(total, rank, gru_bias.reshape(1, -1), memory, agg, held, gru_in, gh)
+    )(total, rank, gru_bias.reshape(1, -1), memory, agg, held, gru_in, gh, fresh)
 
 
 def solution(mesh):

time: 92.9 us -> 84.9 us (0.914)
  Pallas kernels: 92.5 us -> 84.6 us
    pallas_call x1, Pallas kernels: 12.3 us -> 5.22 us  [on_device(): pl.pallas_call(place_kernel, out_shape=jax.ShapeDtypeStruct((N, DM), BF),...]
where the time goes in v4:
time: 84.9 us; the launch traced here: 84.7 us
  Pallas kernels  84.6 us (100%)
    pallas_call x1, Pallas kernels, on_device(): pl.pallas_call(functools.partial(kernel, (D, tm, m, R)), out_shape=[jax.S...  79.4 us
    pallas_call x1, Pallas kernels, on_device(): pl.pallas_call(place_kernel, out_shape=jax.ShapeDtypeStruct((N, DM), BF),...  5.22 us

profile of v4, /device:TPU:0, one launch (start us, length us, event | category | flops | bytes accessed | tf_op | source)
XLA Modules:
  0.0 84.7 jit_solution(17979636010096037972)
XLA Ops:
  0.0 79.4 %shard_map.118 = (bf16[768,1024]{1,0:T(8,128)(2,1)}, f32[768,3072]{1,0:T(8,128)}, bf16[768,1024]{1,0:T(8,128)(2,1)}, s32[1024,128]{1,0:T(8,128)}, s32[8,128]{1,0:T(8,128)}, /*index=5*/bf16[256,1024]{1,0:T(8,128)(2,1)}) custom-call(s32[2,256]{1,0:T(2,128)} %bitcast.10, s32[2,256]{1,0:T(2,128)} %bitcast.11, s32[1,256]{1,0:T(1,128)} %bitcast.12, ...), custom_call_target="tpu_custom_call" | custom-call | tf_op jit(solution)/shard_map/pallas_call | solution.py:516
  79.4 5.2 %shard_map.119 = bf16[1024,1024]{1,0:T(8,128)(2,1)} custom-call(s32[8,128]{1,0:T(8,128)} %get-tuple-element.11.total_ref, s32[1024,128]{1,0:T(8,128)} %get-tuple-element.12.rank_hbm, f32[1,3072]{1,0:T(1,128)} %bitcast.7, bf16[1024,1024]{1,0:T(8,128)(2,1)} %mem_hbm.3, bf16[768,1024]{1,0:T(8,128)(2,1)} %get-tuple-element.13.agg_hbm, ...), custom_call_target="tpu_custom_call" | custom-call | tf_op jit(solution)/shard_map/pallas_call | solution.py:588

commit v5 on v4

--- a/solution.py
+++ b/solution.py
@@ -70,6 +70,7 @@
     HW = DM // HALVES
     tr = QUARTERS * R
     ranks = agg_out.shape[0]
+    nodes = D // tm
     me = lax.axis_index("node") * tm + lax.axis_index("tm")
 
     loads = []
@@ -103,9 +104,13 @@
                 own_sem.at[k + n],
             ).start()
 
-        @pl.loop(1, D)
+        @pl.loop(0, D - 1)
         def _(i):
-            peer = lax.rem(me + i, D)
+            j = i // nodes
+            away = (j + 1) // 2
+            shift = tm // 2 + away - 2 * away * lax.rem(j + 1, 2)
+            peer_node = lax.rem(lax.axis_index("node") + lax.rem(i, nodes) + 1, nodes)
+            peer = peer_node * tm + lax.rem(lax.axis_index("tm") + shift, tm)
             for n, (src, dst, rows) in enumerate(pieces):
                 pltpu.make_async_remote_copy(
                     src_ref=src.at[pl.ds(pl.multiple_of(peer * rows, rows), rows)],

time: 84.9 us -> 84.8 us (level)
  no operation moved by 1% of the time
where the time goes in v5:
time: 84.8 us; the launch traced here: 84.6 us
  Pallas kernels  84.5 us (100%)
    pallas_call x1, Pallas kernels, on_device(): pl.pallas_call(functools.partial(kernel, (D, tm, m, R)), out_shape=[jax.S...  79.2 us
    pallas_call x1, Pallas kernels, on_device(): pl.pallas_call(place_kernel, out_shape=jax.ShapeDtypeStruct((N, DM), BF),...  5.22 us

profile of v5, /device:TPU:0, one launch (start us, length us, event | category | flops | bytes accessed | tf_op | source)
XLA Modules:
  0.0 84.6 jit_solution(7817171273474957329)
XLA Ops:
  0.0 79.2 %shard_map.118 = (bf16[768,1024]{1,0:T(8,128)(2,1)}, f32[768,3072]{1,0:T(8,128)}, bf16[768,1024]{1,0:T(8,128)(2,1)}, s32[1024,128]{1,0:T(8,128)}, s32[8,128]{1,0:T(8,128)}, /*index=5*/bf16[256,1024]{1,0:T(8,128)(2,1)}) custom-call(s32[2,256]{1,0:T(2,128)} %bitcast.10, s32[2,256]{1,0:T(2,128)} %bitcast.11, s32[1,256]{1,0:T(1,128)} %bitcast.12, ...), custom_call_target="tpu_custom_call" | custom-call | tf_op jit(solution)/shard_map/pallas_call | solution.py:521
  79.3 5.2 %shard_map.119 = bf16[1024,1024]{1,0:T(8,128)(2,1)} custom-call(s32[8,128]{1,0:T(8,128)} %get-tuple-element.11.total_ref, s32[1024,128]{1,0:T(8,128)} %get-tuple-element.12.rank_hbm, f32[1,3072]{1,0:T(1,128)} %bitcast.7, bf16[1024,1024]{1,0:T(8,128)(2,1)} %mem_hbm.3, bf16[768,1024]{1,0:T(8,128)(2,1)} %get-tuple-element.13.agg_hbm, ...), custom_call_target="tpu_custom_call" | custom-call | tf_op jit(solution)/shard_map/pallas_call | solution.py:593
